TPU v7x, 512 devices: a whole 4x4x16 slice. The times are simulated.
512 devices in a mesh: chol: 128 (over y, z_lo, x, core), orb: 4 (over z_hi).
Axes of the slice: x: 4, y: 4, z: 16 (z_hi: 4, z_lo: 4; z = z_hi * 4 + z_lo), core: 2. Of those that a mesh axis runs over, the one named last changes fastest.
Arguments:
- half_green: bfloat16 [128, 64, 512], P('chol', None, 'orb'), may hold values from -6 to 6
- rotated_chol: bfloat16 [2560, 64, 512], P('chol', None, 'orb'), may hold values from -0.03125 to 0.03125
- chol_vectors: bfloat16 [2560, 512, 512], P('chol', 'orb'), may hold values from -0.0048828125 to 0.0048828125
- walkers: bfloat16 [128, 64, 512], P('chol', None, 'orb'), may hold values from -6 to 6
- field_levels: int32 [128, 2560], P(None, 'chol'), may hold values from -1 to 1
Outputs:
- force_bias: float32 [128, 2560], P(None, 'chol')
- new_walkers: bfloat16 [128, 64, 512], P('chol', None, 'orb')
Inputs may be any that keep to these rules, and one draw needn't show every extreme that they name: `field_levels`: each entry is -1, 0 or 1.
All inputs are finite; a program needn't handle non-finite values.
Results may differ from a plain program's by a relative error of at most 0.007.
Values may be sent and summed in bfloat16 or wider, within the bound.
No kernel may reach another device: no remote copies, remote signals or barrier semaphores. Data moves between devices by JAX's collectives and lax.ppermute only.
A program may use at most 64 MiB of HBM per device.

v0:
```python
import jax
import jax.numpy as jnp
from jax import lax
from jax.sharding import PartitionSpec as P

LEVEL_SCALE = 1.7320508
TAU_ROOT = 0.2236068


def apply_potential(walker_block, block_fields, chol_flat, own_rows):
    number = walker_block.shape[0]
    block_rows = 16
    num_blocks = number // block_rows
    orbitals = walker_block.shape[1]
    basis = walker_block.shape[2]

    def one_block(operands):
        fields_now, walkers_now = operands
        potential = (
            jnp.dot(fields_now, chol_flat, preferred_element_type=jnp.float32)
            .reshape(block_rows, own_rows, basis)
            .astype(jnp.bfloat16)
        )
        return jnp.einsum(
            "wiq,wpq->wip", walkers_now, potential, preferred_element_type=jnp.float32
        )

    results = lax.map(
        one_block,
        (
            block_fields.reshape(num_blocks, block_rows, block_fields.shape[1]),
            walker_block.reshape(num_blocks, block_rows, orbitals, basis),
        ),
    )
    return results.reshape(number, orbitals, own_rows)


def shards(half_green, rotated_chol, chol_vectors, walkers, field_levels):
    own_rows = chol_vectors.shape[1]
    chol_flat = chol_vectors.reshape(chol_vectors.shape[0], own_rows * chol_vectors.shape[2])
    partial_bias = jnp.einsum(
        "wiq,giq->wg",
        lax.all_gather(half_green, "chol", axis=0, tiled=True),
        rotated_chol,
        preferred_element_type=jnp.float32,
    )
    force_bias = lax.psum(partial_bias, "orb")
    aux_field = (LEVEL_SCALE * field_levels.astype(jnp.float32) - TAU_ROOT * force_bias).astype(
        jnp.bfloat16
    )
    walker_full = lax.all_gather(walkers, "orb", axis=2, tiled=True)
    walker_all = lax.all_gather(walker_full, "chol", axis=0, tiled=True)
    prop_terms = apply_potential(walker_all, aux_field, chol_flat, own_rows)
    own_share = lax.psum_scatter(prop_terms, "chol", scatter_dimension=0, tiled=True)
    new_walkers = (walkers.astype(jnp.float32) - TAU_ROOT * own_share).astype(jnp.bfloat16)
    return (force_bias, new_walkers)


def solution(mesh):
    placed = (
        P("chol", None, "orb"),
        P("chol", None, "orb"),
        P("chol", "orb", None),
        P("chol", None, "orb"),
        P(None, "chol"),
    )
    return jax.shard_map(
        shards,
        mesh=mesh,
        in_specs=placed,
        out_specs=(P(None, "chol"), P("chol", None, "orb")),
        check_vma=False,
    )
```

profile of v0, /device:TPU:1, one launch (start us, length us, event | category | flops | bytes accessed | tf_op | source)
XLA Modules:
  0.0 1175.1 jit_solution(18400375933546843039)
XLA Ops:
  7.2 0.0 all-gather.3.cloned.1.call-start
  7.2 0.7 all-gather.3.cloned.1.call-update
  7.9 0.0 all-gather.5.cloned.1.call-start
  8.0 24.9 %all_gather.10 = bf16[1,64,512]{2,1,0:T(8,128)(2,1)} all-gather(bf16[1,64,128]{2,1,0:T(8,128)(2,1)} %param.10), channel_id=1, replica_groups=mesh['chol'=128,'orb'=4] {'orb'}, dimensions={2}, use_global_device_ids=true | all-gather | bytes 81920 | tf_op jit(solution)/shard_map/all_gather | solution.py:51
  32.8 0.0 all-gather.5.cloned.1.call-update
  32.9 0.0 reduce-scatter.2.cloned.1.call-start
  32.9 2.1 pad
  35.0 1.8 copy.20
  36.8 180.7 %all-gather.3.cloned.1.call-done = bf16[128,64,128]{2,1,0:T(8,128)(2,1)} async-done(((bf16[1,64,128]{2,1,0:T(8,128)(2,1)}), bf16[128,64,128]{2,1,0:T(8,128)(2,1)}) %all-gather.3.cloned.1.call-update) | async-done | bytes 2097168 | tf_op jit(solution)/shard_map/all_gather | solution.py:43
  217.5 3.0 fusion.21
  220.5 21.6 %psum.7 = f32[128,20]{0,1:T(8,128)S(1)} all-reduce(f32[128,20]{0,1:T(8,128)S(1)} %fusion.21), channel_id=1, replica_groups=mesh['chol'=128,'orb'=4] {'orb'}, use_global_device_ids=true, to_apply=%region_0.0 | all-reduce | flops 2560 | bytes 20480 | tf_op jit(solution)/shard_map/psum | solution.py:47
  242.1 0.1 copy.18
  242.2 186.6 %all-gather.5.cloned.1.call-done = bf16[128,64,512]{2,1,0:T(8,128)(2,1)} async-done(((bf16[1,64,512]{2,1,0:T(8,128)(2,1)}), bf16[128,64,512]{2,1,0:T(8,128)(2,1)}) %all-gather.5.cloned.1.call-update) | async-done | bytes 8388624 | tf_op jit(solution)/shard_map/all_gather | solution.py:52
  428.8 58.6 %while.10 = (s32[]{:T(128)}, f32[8,16,64,128]{3,2,1,0:T(8,128)}, bf16[8,16,64,512]{3,2,1,0:T(8,128)(2,1)}, bf16[8,16,20]{2,1,0:T(8,128)(2,1)S(1)}, bf16[20,65536]{1,0:T(8,128)(2,1)S(1)}, /*index=5*/s32[]{:T(128)}) while((s32[]{:T(128)}, f32[8,16,64,128]{3,2,1,0:T(8,128)}, bf16[8,16,64,512]{3,2,1,0:T(8,128)(2,1)}, ...), condition=%wide.region_2.3_spmd, body=%wide.region_1.2_spmd.sunk | while | flops 177209344 | bytes 19928136 | solution.py:28
  428.8 1.1 copy.42
  429.9 0.2 slice_bitcast_fusion.2
  430.1 2.6 fusion.35
  432.7 3.4 fusion.36
  436.1 1.1 copy.42
  437.2 0.2 slice_bitcast_fusion.2
  437.4 2.6 fusion.35
  440.1 3.4 fusion.36
  443.5 1.1 copy.42
  444.6 0.2 slice_bitcast_fusion.2
  444.8 2.6 fusion.35
  447.4 3.4 fusion.36
  450.8 1.1 copy.42
  451.9 0.2 slice_bitcast_fusion.2
  452.1 2.7 fusion.35
  454.7 3.4 fusion.36
  458.1 1.1 copy.42
  459.2 0.2 slice_bitcast_fusion.2
  459.4 2.6 fusion.35
  462.1 3.4 fusion.36
  465.5 1.1 copy.42
  466.6 0.2 slice_bitcast_fusion.2
  466.7 2.6 fusion.35
  469.4 3.4 fusion.36
  472.8 1.1 copy.42
  473.9 0.2 slice_bitcast_fusion.2
  474.1 2.6 fusion.35
  476.7 3.4 fusion.36
  480.1 1.1 copy.42
  481.2 0.2 slice_bitcast_fusion.2
  481.4 2.6 fusion.35
  484.0 3.4 fusion.36
  487.4 679.8 %reduce-scatter.2.cloned.1.call-done = f32[1,64,128]{2,1,0:T(8,128)} async-done(((f32[128,64,128]{2,1,0:T(8,128)}), f32[1,64,128]{2,1,0:T(8,128)}) %reduce-scatter.2.cloned.1.call-update) | async-done | bytes 32784 | tf_op jit(solution)/shard_map/reduce_scatter | solution.py:54
  1167.2 1.4 subtract_convert_fusion
  (11 shorter events, 0.0 us)
Async XLA Ops:
  7.2 210.3 %copy-start = (bf16[20,64,128]{2,1,0:T(8,128)(2,1)S(1)}, bf16[20,64,128]{2,1,0:T(8,128)(2,1)}, u32[]{:S(2)}) copy-start(bf16[20,64,128]{2,1,0:T(8,128)(2,1)} %param.8) | copy-start | bytes 983044
  7.2 210.3 %all-gather.3.cloned.1.call-start = ((), (), s32[]{:S(2)}) async-start(), calls=%async_computation.1 | async-start | bytes 2113536 | tf_op jit(solution)/shard_map/all_gather | solution.py:43
  7.9 420.9 %all-gather.5.cloned.1.call-start = ((), (), s32[]{:S(2)}) async-start(), calls=%async_computation.2 | async-start | bytes 8454144 | tf_op jit(solution)/shard_map/all_gather | solution.py:52
  32.9 1134.4 %reduce-scatter.2.cloned.1.call-start = ((), (), s32[]{:S(2)}) async-start(), calls=%async_computation.3 | async-start | bytes 4227072 | tf_op jit(solution)/shard_map/reduce_scatter | solution.py:54
  35.0 207.0 %copy-start.3 = (s32[128,20]{0,1:T(8,128)S(1)}, s32[128,20]{0,1:T(8,128)}, u32[]{:S(2)}) copy-start(s32[128,20]{0,1:T(8,128)} %param.11) | copy-start | bytes 30724
  242.1 186.7 %copy-start.2 = (f32[128,20]{0,1:T(8,128)}, f32[128,20]{0,1:T(8,128)S(1)}, u32[]{:S(2)}) copy-start(f32[128,20]{0,1:T(8,128)S(1)} %psum.7) | copy-start | bytes 30724
  487.4 679.8 %copy-start.1 = (bf16[1,64,128]{2,1,0:T(8,128)(2,1)S(1)}, bf16[1,64,128]{2,1,0:T(8,128)(2,1)}, u32[]{:S(2)}) copy-start(bf16[1,64,128]{2,1,0:T(8,128)(2,1)} %param.10) | copy-start | bytes 49156
Sparse Core Ops, SparseCore 0:
  10.2 207.2 all-gather.2
  219.6 209.1 all-gather.4
  487.6 679.6 reduce-scatter.1
where the time goes:
time: 1180 us
  waiting for transfers between devices  1050 us (89%)
  matrix products  51.4 us (4%)
  blocking collectives  46.4 us (4%)
  local copies, waits for them, and re-layouts  14.1 us (1%)
  between operations  13.8 us (1%)
    reduce_scatter x1, waiting for transfers between devices, shards(): lax.psum_scatter(prop_terms, 'chol', scatter_dimension=0, tiled=True)  680 us
    all_gather x1, waiting for transfers between devices, shards(): walker_all = lax.all_gather(walker_full, 'chol', axis=0, tiled=True)  187 us
    all_gather x1, waiting for transfers between devices, shards(): lax.all_gather(half_green, 'chol', axis=0, tiled=True)  181 us
    dot_general x8, matrix products, one_block(): jnp.einsum('wiq,wpq->wip', walkers_now, potential, preferred_element_type...  27.3 us
    all_gather x1, blocking collectives, shards(): walker_full = lax.all_gather(walkers, 'orb', axis=2, tiled=True)  24.9 us
  transfers between devices with their start and end apart: 3, of which 3 were waited for; matrix products, arithmetic and copies ran while one was open for 1% of the time, Pallas kernels for 0%

commit v1 on v0

v1 whole, which is shorter than its diff:
```python
import jax
import jax.numpy as jnp
from jax import lax
from jax.sharding import PartitionSpec as P

LEVEL_SCALE = 1.7320508
TAU_ROOT = 0.2236068

SIDE = 4
CORES = 2
CHIPS = SIDE**3
PLANE = SIDE * SIDE
PAD_ROWS = 24


def chol_index(y, z, x, core):
    return ((y * SIDE + z) * SIDE + x) * CORES + core


SAME_CORE = [[CORES * chip + core for chip in range(CHIPS)] for core in range(CORES)]
SAME_PLANE = [
    [chol_index(y, z, x, core) for y in range(SIDE) for x in range(SIDE)]
    for z in range(SIDE)
    for core in range(CORES)
]
OTHER_CORE = [(i, i ^ 1) for i in range(CHIPS * CORES)]


def to_all(block, groups):
    copies = jnp.broadcast_to(block[None], (len(groups[0]),) + block.shape)
    return lax.all_to_all(copies, "chol", 0, 0, axis_index_groups=groups)


def shards(half_green, rotated_chol, chol_vectors, walkers, field_levels):
    f32, bf16 = jnp.float32, jnp.bfloat16
    own, own_rows, basis = chol_vectors.shape
    number = field_levels.shape[0]
    core = lax.axis_index("chol") % CORES
    rows = own_rows // PLANE
    swap = lambda array: lax.ppermute(array, "chol", OTHER_CORE)

    green = to_all(half_green[0], SAME_CORE)
    rotated_other = swap(rotated_chol)

    chol_rows = chol_vectors.reshape(own, PLANE, rows * basis).transpose(1, 0, 2)
    chol_rows = jnp.pad(chol_rows, ((0, 0), (0, PAD_ROWS - own), (0, 0)))
    chol_own = lax.all_to_all(chol_rows, "chol", 0, 0, axis_index_groups=SAME_PLANE)
    chol_own = chol_own.reshape(PLANE * PAD_ROWS, rows * basis)
    chol_other = swap(chol_own)

    levels = field_levels.astype(bf16).reshape(number // CORES, CORES, own)
    levels_own = lax.dynamic_index_in_dim(levels, core, 1, keepdims=False)
    levels_sent = lax.dynamic_index_in_dim(levels, 1 - core, 1, keepdims=False)
    levels_got = swap(levels_sent)
    levels_both = jnp.concatenate([levels_own.T, levels_got.T], axis=1)

    bias_parts = [
        jnp.einsum("giq,wiq->gw", part, green, preferred_element_type=f32)
        for part in (rotated_chol, rotated_other)
    ]
    partial_bias = jnp.concatenate(bias_parts, axis=1).astype(bf16)
    gathered = lax.all_gather(
        jnp.concatenate([partial_bias, walkers[0]], axis=0), "orb", axis=0, tiled=False
    )
    bias = jnp.sum(gathered[:, :own].astype(f32), axis=0)
    walker_full = gathered[:, own:]

    aux_field = (LEVEL_SCALE * levels_both.astype(f32) - TAU_ROOT * bias).astype(bf16)
    aux_field = jnp.pad(aux_field, ((0, PAD_ROWS - own), (0, 0)))
    aux_all = to_all(aux_field, SAME_PLANE).reshape(PLANE * PAD_ROWS, number)
    half = number // CORES
    contract_rows = (((0,), (0,)), ((), ()))
    potential = lax.dot_general(
        aux_all[:, :half], chol_own, contract_rows, preferred_element_type=f32
    ) + lax.dot_general(
        aux_all[:, half:], chol_other, contract_rows, preferred_element_type=f32
    )
    potential = potential.astype(bf16).reshape(CHIPS, rows, basis)
    parts = lax.all_to_all(potential, "chol", 0, 0, axis_index_groups=SAME_CORE)
    parts = parts.reshape(SIDE, SIDE, SIDE, rows, basis)
    total = jnp.sum(parts.astype(f32), axis=1).astype(bf16).reshape(own_rows, basis)
    applied = jnp.einsum(
        "biq,pbq->ip",
        walker_full,
        total.reshape(own_rows, walker_full.shape[0], walker_full.shape[2]),
        preferred_element_type=f32,
    )
    new_walkers = (walkers[0].astype(f32) - TAU_ROOT * applied).astype(bf16)[None]

    bias_got = swap(bias[:, half:])
    bias_own = bias[:, :half]
    pair = jnp.stack(
        [jnp.where(core == 0, bias_own, bias_got), jnp.where(core == 0, bias_got, bias_own)],
        axis=2,
    )
    force_bias = pair.reshape(own, number).T
    return (force_bias, new_walkers)


def solution(mesh):
    placed = (
        P("chol", None, "orb"),
        P("chol", None, "orb"),
        P("chol", "orb", None),
        P("chol", None, "orb"),
        P(None, "chol"),
    )
    return jax.shard_map(
        shards,
        mesh=mesh,
        in_specs=placed,
        out_specs=(P(None, "chol"), P("chol", None, "orb")),
        check_vma=False,
    )
```

time: 1180 us -> 155 us (0.13)
  the two profiles are of different devices: /device:TPU:1 before, /device:TPU:2 now
where the time goes in v1:
time: 155 us; the launch traced here: 154 us
  blocking collectives  80.7 us (52%)
  waiting for transfers between devices  25.5 us (16%)
  starting transfers between devices  22.5 us (15%)
  local copies, waits for them, and re-layouts  14.1 us (9%)
  matrix products  8.39 us (5%)
  other arithmetic  2.39 us (2%)
    all_to_all x1, blocking collectives, shards(): lax.all_to_all(chol_rows, 'chol', 0, 0, axis_index_groups=SAME_PLANE)  46.9 us
    all_gather x1, blocking collectives, shards(): lax.all_gather(jnp.concatenate([partial_bias, walkers[0]], axis=0), 'orb'...  23.2 us
    all_to_all x1, waiting for transfers between devices, to_all(): return lax.all_to_all(copies, 'chol', 0, 0, axis_index_groups=groups)  15.2 us
    all_to_all x1, blocking collectives, to_all(): return lax.all_to_all(copies, 'chol', 0, 0, axis_index_groups=groups)  10.6 us
    all_to_all x1, waiting for transfers between devices, shards(): parts = lax.all_to_all(potential, 'chol', 0, 0, axis_index_groups=SAME_CORE)  9.14 us
    ppermute x4, starting transfers between devices, shards(): swap = lambda array: lax.ppermute(array, 'chol', OTHER_CORE)  8.16 us
    all_to_all x1, starting transfers between devices, to_all(): return lax.all_to_all(copies, 'chol', 0, 0, axis_index_groups=groups)  8.03 us
    all_to_all x1, starting transfers between devices, shards(): parts = lax.all_to_all(potential, 'chol', 0, 0, axis_index_groups=SAME_CORE)  6.3 us
  transfers between devices with their start and end apart: 6, of which 3 were waited for; matrix products, arithmetic and copies ran while one was open for 9% of the time, Pallas kernels for 0%

profile of v1, /device:TPU:2, one launch (start us, length us, event | category | flops | bytes accessed | tf_op | source)
XLA Modules:
  0.0 154.4 jit_solution(7891287787119108547)
XLA Ops:
  0.6 3.9 %reshape.29 = bf16[20,16,4096]{2,1,0:T(8,128)(2,1)S(1)} reshape(bf16[20,128,512]{2,1,0:T(8,128)(2,1)} %param.7) | data formatting | bytes 5242880 | tf_op jit(solution)/shard_map/reshape | solution.py:45
  4.5 1.5 copy.38
  6.0 0.5 pad.9.clone
  6.5 0.0 copy-start
  6.5 46.9 %all_to_all.20 = bf16[16,24,4096]{2,1,0:T(8,128)(2,1)S(1)} all-to-all(bf16[16,24,4096]{2,1,0:T(8,128)(2,1)S(1)} %pad.9.clone), channel_id=1, replica_groups={{0,8,16,24,128,136,144,152,256,264,272,280,384,392,400,408},{4,12,20,28..., dimensions={0} | all-to-all | bytes 6291456 | tf_op jit(solution)/shard_map/all_to_all | solution.py:47
  53.4 0.0 copy-done
  53.4 1.2 broadcast_in_dim.17
  54.7 8.0 %all-to-all-start = ((bf16[64,64,128]{2,1,0:T(8,128)(2,1)}), bf16[64,64,128]{2,1,0:T(8,128)(2,1)}, u32[]{:S(2)}, u32[]{:S(2)}) async-start(bf16[64,64,128]{2,1,0:T(8,128)(2,1)} %broadcast_in_dim.17), calls=%async_computation | async-start | bytes 2097152 | tf_op jit(solution)/shard_map/all_to_all | solution.py:31
  62.7 1.9 %collective-permute-start.3 = (bf16[384,4096]{1,0:T(8,128)(2,1)S(1)}, bf16[384,4096]{1,0:T(8,128)(2,1)}, u32[]{:S(2)}, u32[]{:S(2)}) collective-permute-start(bf16[384,4096]{1,0:T(8,128)(2,1)S(1)} %bitcast.49), channel_id=1, source_target_pairs={{0,4},{4,0},{8,12},{12,8},{16,20},{20,16},{24,28},{28,24},{32,36},... | collective-permute-start | bytes 9437192 | tf_op jit(solution)/shard_map/ppermute | solution.py:40
  64.6 1.2 copy.27
  65.8 2.4 %collective-permute-start = (bf16[20,64,128]{2,0,1:T(8,128)(2,1)S(1)}, bf16[20,64,128]{2,0,1:T(8,128)(2,1)}, u32[]{:S(2)}, u32[]{:S(2)}) collective-permute-start(bf16[20,64,128]{2,0,1:T(8,128)(2,1)S(1)} %copy.27), channel_id=1, source_target_pairs={{0,4},{4,0},{8,12},{12,8},{16,20},{20,16},{24,28},{28,24},{32,36},... | collective-permute-start | bytes 983048 | tf_op jit(solution)/shard_map/ppermute | solution.py:40
  68.3 0.7 convert_element_type.30
  69.0 0.7 copy.32
  69.7 1.5 constant_dynamic-slice_fusion.1
  71.2 0.8 copy.34
  72.1 1.9 %collective-permute-start.2 = (bf16[64,20]{0,1:T(8,128)(2,1)S(1)}, bf16[64,20]{0,1:T(8,128)(2,1)}, u32[]{:S(2)}, u32[]{:S(2)}) collective-permute-start(bf16[64,20]{0,1:T(8,128)(2,1)S(1)} %bitcast.61), channel_id=1, source_target_pairs={{0,4},{4,0},{8,12},{12,8},{16,20},{20,16},{24,28},{28,24},{32,36},... | collective-permute-start | bytes 7688 | tf_op jit(solution)/shard_map/ppermute | solution.py:40
  74.0 0.8 copy.33
  74.9 15.2 %all-to-all-done = bf16[64,64,128]{2,1,0:T(8,128)(2,1)} async-done(((bf16[64,64,128]{2,1,0:T(8,128)(2,1)}), bf16[64,64,128]{2,1,0:T(8,128)(2,1)}, u32[]{:S(2)}, u32[]{:S(2)}) %all-to-all-start) | async-done | bytes 1048608 | tf_op jit(solution)/shard_map/all_to_all | solution.py:31
  90.1 2.2 %fusion.5 = bf16[20,64]{1,0:T(8,128)(2,1)S(1)} fusion(bf16[64,64,128]{2,1,0:T(8,128)(2,1)} %all-to-all-done, bf16[20,64,128]{2,1,0:T(8,128)(2,1)} %param.6), kind=kOutput, calls=%fused_computation.9 | convolution fusion | flops 20972800 | bytes 1378816 | tf_op jit(solution)/shard_map/giq,wiq->gw/dot_general | solution.py:58
  92.3 0.0 collective-permute-done
  92.3 2.1 %fusion.6 = bf16[20,64]{1,0:T(8,128)(2,1)S(1)} fusion(bf16[20,64,128]{2,0,1:T(8,128)(2,1)} %collective-permute-done, bf16[64,64,128]{2,1,0:T(8,128)(2,1)} %all-to-all-done), kind=kOutput, calls=%fused_computation.10 | convolution fusion | flops 20972800 | bytes 1378816 | tf_op jit(solution)/shard_map/giq,wiq->gw/dot_general | solution.py:58
  94.4 0.8 maximum_bitcast_fusion
  95.2 23.2 %all-gather.1 = bf16[4,84,128]{2,1,0:T(8,128)(2,1)S(1)} all-gather(bf16[1,84,128]{2,1,0:T(8,128)(2,1)S(1)} %maximum_bitcast_fusion), channel_id=2, replica_groups=mesh['chol'=128,'orb'=4] {'orb'}, dimensions={0}, use_global_device_ids=true | all-gather | bytes 107520 | tf_op jit(solution)/shard_map/all_gather | solution.py:62
  118.4 0.0 collective-permute-done.2
  118.4 0.8 subtract_convert_fusion
  119.2 10.6 %all_to_all.21 = bf16[16,24,128]{2,1,0:T(8,128)(2,1)S(1)} all-to-all(bf16[16,24,128]{2,1,0:T(8,128)(2,1)S(1)} %broadcast_in_dim.18), channel_id=1, replica_groups={{0,8,16,24,128,136,144,152,256,264,272,280,384,392,400,408},{4,12,20,28..., dimensions={0} | all-to-all | bytes 196608 | tf_op jit(solution)/shard_map/all_to_all | solution.py:31
  129.8 0.7 fusion.11
  130.5 0.0 copy-start.1
  130.5 0.0 collective-permute-done.3
  130.5 2.6 %fusion = bf16[64,4096]{1,0:T(8,128)(2,1)S(1)} fusion(f32[64,4096]{1,0:T(8,128)S(1)} %fusion.11, bf16[384,4096]{1,0:T(8,128)(2,1)} %collective-permute-done.3, bf16[384,128]{1,0:T(8,128)(2,1)S(1)} %bitcast.55), kind=kOutput, calls=%fused_computation.1 | convolution fusion | flops 201850880 | bytes 4816896 | tf_op jit(solution)/shard_map/dot_general | solution.py:75
  133.1 1.0 copy.39
  134.1 6.3 %all-to-all-start.3 = ((bf16[64,8,512]{2,1,0:T(8,128)(2,1)}), bf16[64,8,512]{2,1,0:T(8,128)(2,1)S(1)}, u32[]{:S(2)}, u32[]{:S(2)}) async-start(bf16[64,8,512]{2,1,0:T(8,128)(2,1)} %bitcast.23), calls=%async_computation.3 | async-start | bytes 1048576 | tf_op jit(solution)/shard_map/all_to_all | solution.py:79
  140.4 0.1 slice.26
  140.5 1.9 %collective-permute-start.1 = (f32[20,64]{1,0:T(8,128)S(1)}, f32[20,64]{1,0:T(8,128)S(1)}, u32[]{:S(2)}, u32[]{:S(2)}) collective-permute-start(f32[20,64]{1,0:T(8,128)S(1)} %slice.26), channel_id=1, source_target_pairs={{0,4},{4,0},{8,12},{12,8},{16,20},{20,16},{24,28},{28,24},{32,36},... | collective-permute-start | bytes 15368 | tf_op jit(solution)/shard_map/ppermute | solution.py:40
  142.4 1.1 collective-permute-done.1
  143.5 0.1 copy.31
  143.7 0.7 copy.37
  144.3 9.1 %all-to-all-done.3 = bf16[64,8,512]{2,1,0:T(8,128)(2,1)S(1)} async-done(((bf16[64,8,512]{2,1,0:T(8,128)(2,1)}), bf16[64,8,512]{2,1,0:T(8,128)(2,1)S(1)}, u32[]{:S(2)}, u32[]{:S(2)}) %all-to-all-start.3) | async-done | bytes 524320 | tf_op jit(solution)/shard_map/all_to_all | solution.py:79
  153.5 0.1 reduce_sum.22
  153.6 0.0 copy-done.1
  153.6 0.8 fusion.4
  (6 shorter events, 0.1 us)
Async XLA Ops:
  6.5 47.0 %copy-start = (bf16[1,64,128]{2,1,0:T(8,128)(2,1)S(1)}, bf16[1,64,128]{2,1,0:T(8,128)(2,1)}, u32[]{:S(2)}) copy-start(bf16[1,64,128]{2,1,0:T(8,128)(2,1)} %param.5) | copy-start | bytes 49156
  54.7 35.5 %all-to-all-start = ((bf16[64,64,128]{2,1,0:T(8,128)(2,1)}), bf16[64,64,128]{2,1,0:T(8,128)(2,1)}, u32[]{:S(2)}, u32[]{:S(2)}) async-start(bf16[64,64,128]{2,1,0:T(8,128)(2,1)} %broadcast_in_dim.17), calls=%async_computation | async-start | bytes 2097152 | tf_op jit(solution)/shard_map/all_to_all | solution.py:31
  62.7 67.8 %collective-permute-start.3 = (bf16[384,4096]{1,0:T(8,128)(2,1)S(1)}, bf16[384,4096]{1,0:T(8,128)(2,1)}, u32[]{:S(2)}, u32[]{:S(2)}) collective-permute-start(bf16[384,4096]{1,0:T(8,128)(2,1)S(1)} %bitcast.49), channel_id=1, source_target_pairs={{0,4},{4,0},{8,12},{12,8},{16,20},{20,16},{24,28},{28,24},{32,36},... | collective-permute-start | bytes 9437192 | tf_op jit(solution)/shard_map/ppermute | solution.py:40
  65.8 26.5 %collective-permute-start = (bf16[20,64,128]{2,0,1:T(8,128)(2,1)S(1)}, bf16[20,64,128]{2,0,1:T(8,128)(2,1)}, u32[]{:S(2)}, u32[]{:S(2)}) collective-permute-start(bf16[20,64,128]{2,0,1:T(8,128)(2,1)S(1)} %copy.27), channel_id=1, source_target_pairs={{0,4},{4,0},{8,12},{12,8},{16,20},{20,16},{24,28},{28,24},{32,36},... | collective-permute-start | bytes 983048 | tf_op jit(solution)/shard_map/ppermute | solution.py:40
  72.1 46.3 %collective-permute-start.2 = (bf16[64,20]{0,1:T(8,128)(2,1)S(1)}, bf16[64,20]{0,1:T(8,128)(2,1)}, u32[]{:S(2)}, u32[]{:S(2)}) collective-permute-start(bf16[64,20]{0,1:T(8,128)(2,1)S(1)} %bitcast.61), channel_id=1, source_target_pairs={{0,4},{4,0},{8,12},{12,8},{16,20},{20,16},{24,28},{28,24},{32,36},... | collective-permute-start | bytes 7688 | tf_op jit(solution)/shard_map/ppermute | solution.py:40
  130.5 23.1 %copy-start.1 = (bf16[1,64,128]{2,1,0:T(8,128)(2,1)S(1)}, bf16[1,64,128]{2,1,0:T(8,128)(2,1)}, u32[]{:S(2)}) copy-start(bf16[1,64,128]{2,1,0:T(8,128)(2,1)} %param.8) | copy-start | bytes 49156
  134.1 19.4 %all-to-all-start.3 = ((bf16[64,8,512]{2,1,0:T(8,128)(2,1)}), bf16[64,8,512]{2,1,0:T(8,128)(2,1)S(1)}, u32[]{:S(2)}, u32[]{:S(2)}) async-start(bf16[64,8,512]{2,1,0:T(8,128)(2,1)} %bitcast.23), calls=%async_computation.3 | async-start | bytes 1048576 | tf_op jit(solution)/shard_map/all_to_all | solution.py:79
  140.5 3.1 %collective-permute-start.1 = (f32[20,64]{1,0:T(8,128)S(1)}, f32[20,64]{1,0:T(8,128)S(1)}, u32[]{:S(2)}, u32[]{:S(2)}) collective-permute-start(f32[20,64]{1,0:T(8,128)S(1)} %slice.26), channel_id=1, source_target_pairs={{0,4},{4,0},{8,12},{12,8},{16,20},{20,16},{24,28},{28,24},{32,36},... | collective-permute-start | bytes 15368 | tf_op jit(solution)/shard_map/ppermute | solution.py:40

commit v2 on v0

v2 whole, which is shorter than its diff:
```python
import jax
import jax.numpy as jnp
import numpy as np
from jax import lax
from jax.sharding import PartitionSpec as P

LEVEL_SCALE = 1.7320508
TAU_ROOT = 0.2236068

SIDE = 4
MATES = 4
PLACES = [
    (y, zh, zl, x, core)
    for y in range(SIDE)
    for zh in range(2)
    for zl in range(2)
    for x in range(SIDE)
    for core in range(2)
]


def groups_of(fixed, order):
    found = {}
    for index, place in enumerate(PLACES):
        key = tuple(place[i] for i in fixed)
        found.setdefault(key, []).append((tuple(place[i] for i in order), index))
    return [[index for _, index in sorted(members)] for members in found.values()]


Y, ZH, ZL, X, CORE = range(5)
GREEN = groups_of((ZL, CORE), (Y, ZH, X))
PLANE = groups_of((ZH, ZL, CORE), (Y, X))
BLOCK = groups_of((ZH, CORE), (Y, X, ZL))
HOME = groups_of((CORE,), (ZL, Y, ZH, X))
HOMES = len(HOME[0])
CHIPS = len(PLANE[0])
SHARES = np.zeros((MATES, len(PLACES), len(GREEN[0])), np.float32)
for group in GREEN:
    first = PLACES[group[0]]
    SHARES[first[ZL] * 2 + first[CORE], group, np.arange(len(group))] = 1


def to_mate(array, number):
    step = (number & 1) + (number >> 1) * 2 * SIDE
    return lax.ppermute(array, "chol", [(i, i ^ step) for i in range(len(PLACES))])


def shards(half_green, rotated_chol, chol_vectors, walkers, field_levels):
    f32, bf16 = jnp.float32, jnp.bfloat16
    own, own_rows, basis = chol_vectors.shape
    number = field_levels.shape[0]
    occupied, width = walkers.shape[1], walkers.shape[2]
    share = number // MATES
    rows = own_rows // CHIPS
    index = lax.axis_index("chol")
    core = index % 2
    zl = index // (2 * SIDE) % 2

    def by_number(array):
        array = array.reshape((2, 2) + array.shape[1:])
        array = jnp.where(core == 0, array, jnp.stack([array[:, 1], array[:, 0]], axis=1))
        return jnp.where(zl == 0, array, jnp.stack([array[1], array[0]], axis=0))

    green = jnp.broadcast_to(half_green, (len(GREEN[0]), occupied, width))
    green = lax.all_to_all(green, "chol", 0, 0, axis_index_groups=GREEN)

    levels = jnp.pad(field_levels.astype(bf16).T, ((0, occupied - own), (0, 0)))
    sent = jnp.concatenate([rotated_chol, levels[None]], axis=0)
    held = [sent, to_mate(sent, 1), to_mate(sent, 2)]
    held.append(to_mate(held[2], 1))
    levels = jnp.concatenate([h[own, : own + 1] for h in held], axis=0)
    chosen = lax.dynamic_index_in_dim(jnp.asarray(SHARES, bf16), zl * 2 + core, 0, keepdims=False)
    levels = jnp.dot(levels, chosen, preferred_element_type=f32)

    chol_rows = chol_vectors.reshape(own, CHIPS, 2, rows // 2 * basis).transpose(1, 0, 2, 3)
    chol_rows = chol_rows.reshape(CHIPS, own * 2, rows // 2 * basis)

    green, chol_rows, levels, held = lax.optimization_barrier((green, chol_rows, levels, held))
    chol_mine = lax.all_to_all(chol_rows, "chol", 0, 0, axis_index_groups=PLANE)
    chol_mine = chol_mine.reshape(CHIPS * own * 2, rows // 2 * basis)

    rotated = jnp.concatenate(held, axis=0)
    partial_bias = jnp.einsum("giq,wiq->gw", rotated, green, preferred_element_type=f32)
    partial_bias = jnp.pad(partial_bias.astype(bf16), ((0, 0), (0, width - share)))
    gathered = lax.all_gather(
        jnp.concatenate([walkers[0], partial_bias], axis=0), "orb", axis=0, tiled=False
    )
    bias = jnp.sum(gathered[:, occupied:, :share].astype(f32), axis=0)
    walker_full = gathered[:, :occupied]
    bias, chol_mine, walker_full = lax.optimization_barrier((bias, chol_mine, walker_full))

    aux_field = (LEVEL_SCALE * levels - TAU_ROOT * bias).astype(bf16)
    aux_field = aux_field.reshape(2, 2, own + 1, share)[:, :, :own]
    aux_field = jnp.where(zl == 0, aux_field, jnp.stack([aux_field[1], aux_field[0]]))
    zero = jnp.zeros_like(aux_field)
    aux_field = jnp.stack(
        [jnp.concatenate([aux_field, zero], axis=3), jnp.concatenate([zero, aux_field], axis=3)],
        axis=3,
    ).reshape(2, 2 * own * 2, 2 * share)
    aux_sent = jnp.broadcast_to(aux_field[None], (CHIPS,) + aux_field.shape)
    aux_sent = aux_sent.reshape((CHIPS * 2,) + aux_field.shape[1:])
    aux_all = lax.all_to_all(aux_sent, "chol", 0, 0, axis_index_groups=BLOCK)
    aux_all = aux_all.reshape(CHIPS, 2, 2, own * 2, 2 * share)
    aux_all = jnp.concatenate([aux_all[:, 0], aux_all[:, 1]], axis=3)
    chol_others = to_mate(chol_mine, 1)
    potential = sum(
        lax.dot_general(
            aux_all[:, i].reshape(CHIPS * own * 2, 4 * share),
            part,
            (((0,), (0,)), ((), ())),
            preferred_element_type=f32,
        )
        for i, part in enumerate((chol_mine, chol_others))
    )
    potential = potential.astype(bf16).reshape(2, 2, share, rows // 2 * basis)
    potential = potential.transpose(0, 2, 1, 3).reshape(HOMES, rows, basis)
    parts = lax.all_to_all(potential, "chol", 0, 0, axis_index_groups=HOME)
    parts = parts.reshape(2, SIDE, 2, SIDE, rows, basis)
    total = jnp.sum(parts.astype(f32), axis=(0, 2)).astype(bf16)

    applied = jnp.einsum(
        "biq,pbq->ip",
        walker_full,
        total.reshape(own_rows, basis // width, width),
        preferred_element_type=f32,
    )
    new_walkers = (walkers[0].astype(f32) - TAU_ROOT * applied).astype(bf16)[None]

    bias = bias.reshape(MATES, own + 1, share)[:, :own]
    bias = [bias[0]] + [to_mate(bias[r], r) for r in range(1, MATES)]
    bias = by_number(jnp.stack(bias)).reshape(2, 2, own, SIDE, 2, SIDE)
    force_bias = bias.transpose(3, 4, 0, 5, 1, 2).reshape(number, own)
    return (force_bias, new_walkers)


def solution(mesh):
    placed = (
        P("chol", None, "orb"),
        P("chol", None, "orb"),
        P("chol", "orb", None),
        P("chol", None, "orb"),
        P(None, "chol"),
    )
    return jax.shard_map(
        shards,
        mesh=mesh,
        in_specs=placed,
        out_specs=(P(None, "chol"), P("chol", None, "orb")),
        check_vma=False,
    )
```

time: 1180 us -> 149 us (0.13)
  the two profiles are of different devices: /device:TPU:1 before, /device:TPU:128 now
where the time goes in v2:
time: 149 us; the launch traced here: 148 us
  starting transfers between devices  42.8 us (29%)
  waiting for transfers between devices  37.9 us (25%)
  blocking collectives  37.8 us (25%)
  local copies, waits for them, and re-layouts  20.3 us (14%)
  matrix products  6.74 us (5%)
    all_gather x1, blocking collectives, shards(): lax.all_gather(jnp.concatenate([walkers[0], partial_bias], axis=0), 'orb'...  20.6 us
    all_to_all x1, waiting for transfers between devices, shards(): chol_mine = lax.all_to_all(chol_rows, 'chol', 0, 0, axis_index_groups=PLANE)  18 us
    all_to_all x1, blocking collectives, shards(): aux_all = lax.all_to_all(aux_sent, 'chol', 0, 0, axis_index_groups=BLOCK)  17.2 us
    ppermute x7, starting transfers between devices, to_mate(): lax.ppermute(array, 'chol', [(i, i ^ step) for i in range(len(PLACES))])  17.2 us
    ppermute x7, waiting for transfers between devices, to_mate(): lax.ppermute(array, 'chol', [(i, i ^ step) for i in range(len(PLACES))])  12.1 us
    all_to_all x1, starting transfers between devices, shards(): green = lax.all_to_all(green, 'chol', 0, 0, axis_index_groups=GREEN)  10 us
    all_to_all x1, starting transfers between devices, shards(): parts = lax.all_to_all(potential, 'chol', 0, 0, axis_index_groups=HOME)  8.68 us
    all_to_all x1, waiting for transfers between devices, shards(): parts = lax.all_to_all(potential, 'chol', 0, 0, axis_index_groups=HOME)  7.7 us
  transfers between devices with their start and end apart: 10, of which 6 were waited for; matrix products, arithmetic and copies ran while one was open for 13% of the time, Pallas kernels for 0%

profile of v2, /device:TPU:128, one launch (start us, length us, event | category | flops | bytes accessed | tf_op | source)
XLA Modules:
  0.0 148.1 jit_solution(7337592598240578758)
XLA Ops:
  0.6 1.8 %broadcast_in_dim.22 = bf16[32,64,128]{2,1,0:T(8,128)(2,1)} broadcast(bf16[64,128]{1,0:T(8,128)(2,1)} %bitcast.115), dimensions={1,2} | broadcast | bytes 540672 | tf_op jit(solution)/shard_map/broadcast_in_dim | solution.py:64
  2.4 10.0 %all-to-all-start = ((bf16[32,64,128]{2,1,0:T(8,128)(2,1)}), bf16[32,64,128]{2,1,0:T(8,128)(2,1)S(1)}, u32[]{:S(2)}, u32[]{:S(2)}) async-start(bf16[32,64,128]{2,1,0:T(8,128)(2,1)} %broadcast_in_dim.22), calls=%async_computation | async-start | bytes 1048576 | tf_op jit(solution)/shard_map/all_to_all | solution.py:65
  12.5 0.7 convert_bitcast_fusion
  13.2 1.2 copy.156
  14.4 0.1 pad_maximum_fusion
  14.5 3.8 %collective-permute-start.1 = (bf16[21,64,128]{2,0,1:T(8,128)(2,1)S(1)}, bf16[21,64,128]{2,0,1:T(8,128)(2,1)}, u32[]{:S(2)}, u32[]{:S(2)}) collective-permute-start(bf16[21,64,128]{2,0,1:T(8,128)(2,1)S(1)} %pad_maximum_fusion), channel_id=1, source_target_pairs={{0,32},{4,36},{8,40},{12,44},{16,48},{20,52},{24,56},{28,60},{32,0... | collective-permute-start | bytes 1032200 | tf_op jit(solution)/shard_map/ppermute | solution.py:45
  18.4 1.9 %collective-permute-start = (bf16[21,64,128]{2,0,1:T(8,128)(2,1)S(1)}, bf16[21,64,128]{2,0,1:T(8,128)(2,1)}, u32[]{:S(2)}, u32[]{:S(2)}) collective-permute-start(bf16[21,64,128]{2,0,1:T(8,128)(2,1)S(1)} %pad_maximum_fusion), channel_id=1, source_target_pairs={{0,4},{4,0},{8,12},{12,8},{16,20},{20,16},{24,28},{28,24},{32,36},... | collective-permute-start | bytes 1032200 | tf_op jit(solution)/shard_map/ppermute | solution.py:45
  20.3 11.2 %collective-permute-done.1 = bf16[21,64,128]{2,0,1:T(8,128)(2,1)} collective-permute-done((bf16[21,64,128]{2,0,1:T(8,128)(2,1)S(1)}, bf16[21,64,128]{2,0,1:T(8,128)(2,1)}, u32[]{:S(2)}, u32[]{:S(2)}) %collective-permute-start.1) | collective-permute-done | bytes 344096 | tf_op jit(solution)/shard_map/ppermute | solution.py:45
  31.4 1.9 %collective-permute-start.2 = (bf16[21,64,128]{2,0,1:T(8,128)(2,1)}, bf16[21,64,128]{2,0,1:T(8,128)(2,1)}, u32[]{:S(2)}, u32[]{:S(2)}) collective-permute-start(bf16[21,64,128]{2,0,1:T(8,128)(2,1)} %collective-permute-done.1), channel_id=1, source_target_pairs={{0,4},{4,0},{8,12},{12,8},{16,20},{20,16},{24,28},{28,24},{32,36},... | collective-permute-start | bytes 1032200 | tf_op jit(solution)/shard_map/ppermute | solution.py:45
  33.4 3.0 %reshape.52 = bf16[20,16,2,2048]{3,2,1,0:T(2,128)(2,1)} reshape(bf16[20,128,512]{2,1,0:T(8,128)(2,1)S(1)} %copy-done) | data formatting | bytes 5242880 | tf_op jit(solution)/shard_map/reshape | solution.py:75
  36.4 2.9 %copy.155 = bf16[16,20,2,2048]{3,0,2,1:T(8,128)(2,1)S(1)} copy(bf16[16,20,2,2048]{3,2,0,1:T(2,128)(2,1)} %bitcast.96) | data formatting | bytes 5242880 | tf_op jit(solution)/shard_map/transpose | solution.py:75
  39.3 0.8 slice.93
  40.1 0.8 slice.92
  40.9 0.8 slice.94
  41.8 1.6 %fusion.27 = f32[84,32]{0,1:T(8,128)} fusion(bf16[4,128,32]{2,1,0:T(8,128)(2,1)} %constant.56.clone, s32[]{:T(128)S(6)} %select_n.52, bf16[21,128]{1,0:T(8,128)(2,1)S(1)} %bitcast.124, bf16[21,128]{1,0:T(8,128)(2,1)S(1)} %bitcast.122, bf16[21,128]{1,0:T(8,128)(2,1)S(1)} %bitcast.123, bf16[21,128]{1,0:T(8,128)(2,1)S(1)} %slice_bitcast_fusion.2), kind=kOutput, calls=%fused_computation.41 | convolution fusion | flops 774144 | bytes 65028 | tf_op jit(solution)/shard_map/dot_general | solution.py:73
  43.3 2.9 %copy.160 = bf16[16,40,2048]{2,1,0:T(8,128)(2,1)} copy(bf16[16,40,2048]{2,0,1:T(8,128)(2,1)S(1)} %bitcast.95) | data formatting | bytes 5242880 | tf_op jit(solution)/shard_map/optimization_barrier | solution.py:78
  46.3 6.9 %all-to-all-start.1 = ((bf16[16,40,2048]{2,1,0:T(8,128)(2,1)}), bf16[16,40,2048]{2,1,0:T(8,128)(2,1)S(1)}, u32[]{:S(2)}, u32[]{:S(2)}) async-start(bf16[16,40,2048]{2,1,0:T(8,128)(2,1)} %copy.160), calls=%async_computation.1 | async-start | bytes 5242880 | tf_op jit(solution)/shard_map/all_to_all | solution.py:79
  53.2 0.7 copy.154
  53.9 2.1 %fusion.16 = bf16[84,32]{0,1:T(8,128)(2,1)S(1)} fusion(bf16[21,64,128]{2,0,1:T(8,128)(2,1)} %collective-permute-done.2, bf16[21,64,128]{2,0,1:T(8,128)(2,1)} %collective-permute-done.1, bf16[21,64,128]{2,0,1:T(8,128)(2,1)} %collective-permute-done, bf16[21,64,128]{2,0,1:T(8,128)(2,1)S(1)} %pad_maximum_fusion, bf16[32,64,128]{2,1,0:T(8,128)(2,1)S(1)} %all-to-all-done), kind=kOutput, calls=%fused_computation.16 | convolution fusion | flops 49547904 | bytes 1905920 | tf_op jit(solution)/shard_map/giq,wiq->gw/dot_general | solution.py:83
  56.1 0.1 copy.159
  56.2 20.6 %all-gather.1 = bf16[4,148,128]{2,1,0:T(8,128)(2,1)S(1)} all-gather(bf16[1,148,128]{2,1,0:T(8,128)(2,1)S(1)} %copy.159), channel_id=2, replica_groups=mesh['chol'=128,'orb'=4] {'orb'}, dimensions={0}, use_global_device_ids=true | all-gather | bytes 189440 | tf_op jit(solution)/shard_map/all_gather | solution.py:85
  76.8 18.0 %all-to-all-done.1 = bf16[16,40,2048]{2,1,0:T(8,128)(2,1)S(1)} async-done(((bf16[16,40,2048]{2,1,0:T(8,128)(2,1)}), bf16[16,40,2048]{2,1,0:T(8,128)(2,1)S(1)}, u32[]{:S(2)}, u32[]{:S(2)}) %all-to-all-start.1) | async-done | bytes 2621472 | tf_op jit(solution)/shard_map/all_to_all | solution.py:79
  95.0 0.1 reshape.59
  95.0 1.9 %collective-permute-start.6 = (bf16[640,2048]{1,0:T(8,128)(2,1)S(1)}, bf16[640,2048]{1,0:T(8,128)(2,1)}, u32[]{:S(2)}, u32[]{:S(2)}) collective-permute-start(bf16[640,2048]{1,0:T(8,128)(2,1)S(1)} %bitcast.93), channel_id=1, source_target_pairs={{0,4},{4,0},{8,12},{12,8},{16,20},{20,16},{24,28},{28,24},{32,36},... | collective-permute-start | bytes 7864328 | tf_op jit(solution)/shard_map/ppermute | solution.py:45
  97.2 0.1 copy.172
  97.3 0.1 copy.171
  97.4 0.1 pad_maximum_fusion.3
  97.6 0.1 copy.173
  97.7 0.1 broadcast_in_dim.25
  97.8 17.2 %all_to_all.20 = bf16[32,80,64]{1,2,0:T(8,128)(2,1)} all-to-all(bf16[32,80,64]{1,2,0:T(8,128)(2,1)S(1)} %bitcast.100), channel_id=1, replica_groups={{0,32,8,40,16,48,24,56,128,160,136,168,144,176,152,184,256,288,264,296,..., dimensions={0} | all-to-all | bytes 655360 | tf_op jit(solution)/shard_map/all_to_all | solution.py:102
  115.0 1.3 copy.174
  116.4 0.2 pad_maximum_fusion.1
  116.6 0.6 fusion.44
  117.2 2.4 %fusion = bf16[128,2048]{1,0:T(8,128)(2,1)S(1)} fusion(f32[128,2048]{1,0:T(8,128)S(1)} %fusion.44, bf16[640,128]{1,0:T(8,128)(2,1)S(1)} %bitcast.105, bf16[640,2048]{1,0:T(8,128)(2,1)} %collective-permute-done.6), kind=kOutput, calls=%fused_computation.1 | convolution fusion | flops 336068608 | bytes 4358144 | tf_op jit(solution)/shard_map/dot_general | solution.py:107
  119.6 0.5 copy.206
  120.2 0.9 reshape.63
  121.1 8.7 %all-to-all-start.3 = ((bf16[64,8,512]{2,1,0:T(8,128)(2,1)}), bf16[64,8,512]{2,1,0:T(8,128)(2,1)S(1)}, u32[]{:S(2)}, u32[]{:S(2)}) async-start(bf16[64,8,512]{2,1,0:T(8,128)(2,1)} %reshape.63), calls=%async_computation.3 | async-start | bytes 1048576 | tf_op jit(solution)/shard_map/all_to_all | solution.py:117
  129.8 0.1 reshape.55
  129.9 1.9 %collective-permute-start.5 = (f32[20,32]{0,1:T(8,128)S(1)}, f32[20,32]{0,1:T(8,128)S(1)}, u32[]{:S(2)}, u32[]{:S(2)}) collective-permute-start(f32[20,32]{0,1:T(8,128)S(1)} %bitcast.120), channel_id=1, source_target_pairs={{0,36},{4,32},{8,44},{12,40},{16,52},{20,48},{24,60},{28,56},{32,4... | collective-permute-start | bytes 7688 | tf_op jit(solution)/shard_map/ppermute | solution.py:45
  131.9 3.6 %collective-permute-start.4 = (f32[20,32]{0,1:T(8,128)S(1)}, f32[20,32]{0,1:T(8,128)S(1)}, u32[]{:S(2)}, u32[]{:S(2)}) collective-permute-start(f32[20,32]{0,1:T(8,128)S(1)} %bitcast.118), channel_id=1, source_target_pairs={{0,32},{4,36},{8,40},{12,44},{16,48},{20,52},{24,56},{28,60},{32,0... | collective-permute-start | bytes 7688 | tf_op jit(solution)/shard_map/ppermute | solution.py:45
  135.5 2.1 %collective-permute-start.3 = (f32[20,32]{0,1:T(8,128)S(1)}, f32[20,32]{0,1:T(8,128)S(1)}, u32[]{:S(2)}, u32[]{:S(2)}) collective-permute-start(f32[20,32]{0,1:T(8,128)S(1)} %bitcast.116), channel_id=1, source_target_pairs={{0,4},{4,0},{8,12},{12,8},{16,20},{20,16},{24,28},{28,24},{32,36},... | collective-permute-start | bytes 7688 | tf_op jit(solution)/shard_map/ppermute | solution.py:45
  137.6 0.1 collective-permute-done.5
  137.6 0.2 collective-permute-done.4
  137.8 0.7 collective-permute-done.3
  138.7 0.7 copy.179
  139.4 7.7 %all-to-all-done.3 = bf16[64,8,512]{2,1,0:T(8,128)(2,1)S(1)} async-done(((bf16[64,8,512]{2,1,0:T(8,128)(2,1)}), bf16[64,8,512]{2,1,0:T(8,128)(2,1)S(1)}, u32[]{:S(2)}, u32[]{:S(2)}) %all-to-all-start.3) | async-done | bytes 524320 | tf_op jit(solution)/shard_map/all_to_all | solution.py:117
  147.2 0.2 fusion.12
  147.4 0.7 copy.180
  (43 shorter events, 0.8 us)
Async XLA Ops:
  0.6 32.8 %copy-start = (bf16[20,128,512]{2,1,0:T(8,128)(2,1)S(1)}, bf16[20,128,512]{2,1,0:T(8,128)(2,1)}, u32[]{:S(2)}) copy-start(bf16[20,128,512]{2,1,0:T(8,128)(2,1)} %param.8) | copy-start | bytes 7864324
  2.4 40.9 %all-to-all-start = ((bf16[32,64,128]{2,1,0:T(8,128)(2,1)}), bf16[32,64,128]{2,1,0:T(8,128)(2,1)S(1)}, u32[]{:S(2)}, u32[]{:S(2)}) async-start(bf16[32,64,128]{2,1,0:T(8,128)(2,1)} %broadcast_in_dim.22), calls=%async_computation | async-start | bytes 1048576 | tf_op jit(solution)/shard_map/all_to_all | solution.py:65
  14.5 16.9 %collective-permute-start.1 = (bf16[21,64,128]{2,0,1:T(8,128)(2,1)S(1)}, bf16[21,64,128]{2,0,1:T(8,128)(2,1)}, u32[]{:S(2)}, u32[]{:S(2)}) collective-permute-start(bf16[21,64,128]{2,0,1:T(8,128)(2,1)S(1)} %pad_maximum_fusion), channel_id=1, source_target_pairs={{0,32},{4,36},{8,40},{12,44},{16,48},{20,52},{24,56},{28,60},{32,0... | collective-permute-start | bytes 1032200 | tf_op jit(solution)/shard_map/ppermute | solution.py:45
  18.4 21.8 %collective-permute-start = (bf16[21,64,128]{2,0,1:T(8,128)(2,1)S(1)}, bf16[21,64,128]{2,0,1:T(8,128)(2,1)}, u32[]{:S(2)}, u32[]{:S(2)}) collective-permute-start(bf16[21,64,128]{2,0,1:T(8,128)(2,1)S(1)} %pad_maximum_fusion), channel_id=1, source_target_pairs={{0,4},{4,0},{8,12},{12,8},{16,20},{20,16},{24,28},{28,24},{32,36},... | collective-permute-start | bytes 1032200 | tf_op jit(solution)/shard_map/ppermute | solution.py:45
  31.4 9.5 %collective-permute-start.2 = (bf16[21,64,128]{2,0,1:T(8,128)(2,1)}, bf16[21,64,128]{2,0,1:T(8,128)(2,1)}, u32[]{:S(2)}, u32[]{:S(2)}) collective-permute-start(bf16[21,64,128]{2,0,1:T(8,128)(2,1)} %collective-permute-done.1), channel_id=1, source_target_pairs={{0,4},{4,0},{8,12},{12,8},{16,20},{20,16},{24,28},{28,24},{32,36},... | collective-permute-start | bytes 1032200 | tf_op jit(solution)/shard_map/ppermute | solution.py:45
  46.3 7.0 %copy-start.4 = (bf16[1,64,128]{2,1,0:T(8,128)(2,1)S(1)}, bf16[1,64,128]{2,1,0:T(8,128)(2,1)}, u32[]{:S(2)}) copy-start(bf16[1,64,128]{2,1,0:T(8,128)(2,1)} %param.9) | copy-start | bytes 49156
  46.3 48.6 %all-to-all-start.1 = ((bf16[16,40,2048]{2,1,0:T(8,128)(2,1)}), bf16[16,40,2048]{2,1,0:T(8,128)(2,1)S(1)}, u32[]{:S(2)}, u32[]{:S(2)}) async-start(bf16[16,40,2048]{2,1,0:T(8,128)(2,1)} %copy.160), calls=%async_computation.1 | async-start | bytes 5242880 | tf_op jit(solution)/shard_map/all_to_all | solution.py:79
  53.9 2.1 %copy-start.2 = (bf16[1,64,128]{1,2,0:T(8,128)(2,1)S(1)}, bf16[1,64,128]{1,2,0:T(8,128)(2,1)}, u32[]{:S(2)}) copy-start(bf16[1,64,128]{1,2,0:T(8,128)(2,1)} %copy.154) | copy-start | bytes 49156
  53.9 41.0 %copy-start.5 = (f32[84,32]{0,1:T(8,128)S(1)}, f32[84,32]{0,1:T(8,128)}, u32[]{:S(2)}) copy-start(f32[84,32]{0,1:T(8,128)} %fusion.27) | copy-start | bytes 32260
  76.8 39.6 %copy-start.1 = (bf16[4,148,128]{2,1,0:T(8,128)(2,1)}, bf16[4,148,128]{2,1,0:T(8,128)(2,1)S(1)}, u32[]{:S(2)}) copy-start(bf16[4,148,128]{2,1,0:T(8,128)(2,1)S(1)} %all-gather.1) | copy-start | bytes 454660
  95.0 22.2 %collective-permute-start.6 = (bf16[640,2048]{1,0:T(8,128)(2,1)S(1)}, bf16[640,2048]{1,0:T(8,128)(2,1)}, u32[]{:S(2)}, u32[]{:S(2)}) collective-permute-start(bf16[640,2048]{1,0:T(8,128)(2,1)S(1)} %bitcast.93), channel_id=1, source_target_pairs={{0,4},{4,0},{8,12},{12,8},{16,20},{20,16},{24,28},{28,24},{32,36},... | collective-permute-start | bytes 7864328 | tf_op jit(solution)/shard_map/ppermute | solution.py:45
  119.6 27.6 %slice-start = ((bf16[4,148,128]{2,1,0:T(8,128)(2,1)}), bf16[4,64,128]{2,1,0:T(8,128)(2,1)S(1)}, s32[]{:S(2)}) async-start(bf16[4,148,128]{2,1,0:T(8,128)(2,1)} %copy-done.1), calls=%async_computation.4 | async-start | bytes 131072 | tf_op jit(solution)/shard_map/slice | solution.py:89
  119.6 27.6 %copy-start.3 = (bf16[1,64,128]{1,2,0:T(8,128)(2,1)S(1)}, bf16[1,64,128]{1,2,0:T(8,128)(2,1)}, u32[]{:S(2)}) copy-start(bf16[1,64,128]{1,2,0:T(8,128)(2,1)} %copy.154) | copy-start | bytes 49156
  121.1 26.0 %all-to-all-start.3 = ((bf16[64,8,512]{2,1,0:T(8,128)(2,1)}), bf16[64,8,512]{2,1,0:T(8,128)(2,1)S(1)}, u32[]{:S(2)}, u32[]{:S(2)}) async-start(bf16[64,8,512]{2,1,0:T(8,128)(2,1)} %reshape.63), calls=%async_computation.3 | async-start | bytes 1048576 | tf_op jit(solution)/shard_map/all_to_all | solution.py:117
  129.9 7.7 %collective-permute-start.5 = (f32[20,32]{0,1:T(8,128)S(1)}, f32[20,32]{0,1:T(8,128)S(1)}, u32[]{:S(2)}, u32[]{:S(2)}) collective-permute-start(f32[20,32]{0,1:T(8,128)S(1)} %bitcast.120), channel_id=1, source_target_pairs={{0,36},{4,32},{8,44},{12,40},{16,52},{20,48},{24,60},{28,56},{32,4... | collective-permute-start | bytes 7688 | tf_op jit(solution)/shard_map/ppermute | solution.py:45
  131.9 6.0 %collective-permute-start.4 = (f32[20,32]{0,1:T(8,128)S(1)}, f32[20,32]{0,1:T(8,128)S(1)}, u32[]{:S(2)}, u32[]{:S(2)}) collective-permute-start(f32[20,32]{0,1:T(8,128)S(1)} %bitcast.118), channel_id=1, source_target_pairs={{0,32},{4,36},{8,40},{12,44},{16,48},{20,52},{24,56},{28,60},{32,0... | collective-permute-start | bytes 7688 | tf_op jit(solution)/shard_map/ppermute | solution.py:45
  135.5 3.1 %collective-permute-start.3 = (f32[20,32]{0,1:T(8,128)S(1)}, f32[20,32]{0,1:T(8,128)S(1)}, u32[]{:S(2)}, u32[]{:S(2)}) collective-permute-start(f32[20,32]{0,1:T(8,128)S(1)} %bitcast.116), channel_id=1, source_target_pairs={{0,4},{4,0},{8,12},{12,8},{16,20},{20,16},{24,28},{28,24},{32,36},... | collective-permute-start | bytes 7688 | tf_op jit(solution)/shard_map/ppermute | solution.py:45

commit v3 on v2

--- a/solution.py
+++ b/solution.py
@@ -67,17 +67,18 @@
     levels = jnp.pad(field_levels.astype(bf16).T, ((0, occupied - own), (0, 0)))
     sent = jnp.concatenate([rotated_chol, levels[None]], axis=0)
     held = [sent, to_mate(sent, 1), to_mate(sent, 2)]
+
+    chol_rows = chol_vectors.reshape(own, CHIPS, 2, rows // 2 * basis).transpose(1, 0, 2, 3)
+    chol_rows = chol_rows.reshape(CHIPS, own * 2, rows // 2 * basis)
+
+    green, chol_rows, held = lax.optimization_barrier((green, chol_rows, held))
+    chol_mine = lax.all_to_all(chol_rows, "chol", 0, 0, axis_index_groups=PLANE)
+    chol_mine = chol_mine.reshape(CHIPS * own * 2, rows // 2 * basis)
+
     held.append(to_mate(held[2], 1))
     levels = jnp.concatenate([h[own, : own + 1] for h in held], axis=0)
     chosen = lax.dynamic_index_in_dim(jnp.asarray(SHARES, bf16), zl * 2 + core, 0, keepdims=False)
     levels = jnp.dot(levels, chosen, preferred_element_type=f32)
-
-    chol_rows = chol_vectors.reshape(own, CHIPS, 2, rows // 2 * basis).transpose(1, 0, 2, 3)
-    chol_rows = chol_rows.reshape(CHIPS, own * 2, rows // 2 * basis)
-
-    green, chol_rows, levels, held = lax.optimization_barrier((green, chol_rows, levels, held))
-    chol_mine = lax.all_to_all(chol_rows, "chol", 0, 0, axis_index_groups=PLANE)
-    chol_mine = chol_mine.reshape(CHIPS * own * 2, rows // 2 * basis)
 
     rotated = jnp.concatenate(held, axis=0)
     partial_bias = jnp.einsum("giq,wiq->gw", rotated, green, preferred_element_type=f32)

time: 149 us -> 137 us (0.919)
  waiting for transfers between devices: 37.9 us -> 28.5 us
  starting transfers between devices: 42.8 us -> 41 us
    all_to_all x1, waiting for transfers between devices: 18 us -> 11.7 us  [shards(): chol_mine = lax.all_to_all(chol_rows, 'chol', 0, 0, axis_index_groups=PLANE)]
    all_to_all x1, starting transfers between devices: 8.68 us -> 6.58 us  [shards(): parts = lax.all_to_all(potential, 'chol', 0, 0, axis_index_groups=HOME)]
    all_to_all x1, waiting for transfers between devices: 7.7 us -> 5.65 us  [shards(): parts = lax.all_to_all(potential, 'chol', 0, 0, axis_index_groups=HOME)]
    unnamed x22 -> x20, local copies, waits for them, and re-layouts: 3.44 us -> 4.04 us
  transfers between devices with their start and end apart: 10 -> 10, of which waited for: 6 -> 4; matrix products, arithmetic and copies ran while one was open for 13% -> 13% of each run, Pallas kernels for 0% -> 0%
where the time goes in v3:
time: 137 us; the launch traced here: 136 us
  starting transfers between devices  41 us (30%)
  blocking collectives  36.8 us (27%)
  waiting for transfers between devices  28.5 us (21%)
  local copies, waits for them, and re-layouts  20.9 us (15%)
  matrix products  6.15 us (4%)
  other arithmetic  1.43 us (1%)
    all_gather x1, blocking collectives, shards(): lax.all_gather(jnp.concatenate([walkers[0], partial_bias], axis=0), 'orb'...  20 us
    ppermute x7, starting transfers between devices, to_mate(): lax.ppermute(array, 'chol', [(i, i ^ step) for i in range(len(PLACES))])  17.2 us
    all_to_all x1, blocking collectives, shards(): aux_all = lax.all_to_all(aux_sent, 'chol', 0, 0, axis_index_groups=BLOCK)  16.8 us
    all_to_all x1, waiting for transfers between devices, shards(): chol_mine = lax.all_to_all(chol_rows, 'chol', 0, 0, axis_index_groups=PLANE)  11.7 us
    ppermute x7, waiting for transfers between devices, to_mate(): lax.ppermute(array, 'chol', [(i, i ^ step) for i in range(len(PLACES))])  11.2 us
    all_to_all x1, starting transfers between devices, shards(): green = lax.all_to_all(green, 'chol', 0, 0, axis_index_groups=GREEN)  10 us
    all_to_all x1, starting transfers between devices, shards(): chol_mine = lax.all_to_all(chol_rows, 'chol', 0, 0, axis_index_groups=PLANE)  7.22 us
    all_to_all x1, starting transfers between devices, shards(): parts = lax.all_to_all(potential, 'chol', 0, 0, axis_index_groups=HOME)  6.58 us
  transfers between devices with their start and end apart: 10, of which 4 were waited for; matrix products, arithmetic and copies ran while one was open for 13% of the time, Pallas kernels for 0%

profile of v3, /device:TPU:128, one launch (start us, length us, event | category | flops | bytes accessed | tf_op | source)
XLA Modules:
  0.0 136.0 jit_solution(14618471470365144709)
XLA Ops:
  0.6 1.8 %broadcast_in_dim.22 = bf16[32,64,128]{2,1,0:T(8,128)(2,1)} broadcast(bf16[64,128]{1,0:T(8,128)(2,1)} %bitcast.114), dimensions={1,2} | broadcast | bytes 540672 | tf_op jit(solution)/shard_map/broadcast_in_dim | solution.py:64
  2.4 10.0 %all-to-all-start = ((bf16[32,64,128]{2,1,0:T(8,128)(2,1)}), bf16[32,64,128]{2,1,0:T(8,128)(2,1)S(1)}, u32[]{:S(2)}, u32[]{:S(2)}) async-start(bf16[32,64,128]{2,1,0:T(8,128)(2,1)} %broadcast_in_dim.22), calls=%async_computation | async-start | bytes 1048576 | tf_op jit(solution)/shard_map/all_to_all | solution.py:65
  12.5 1.2 copy.158
  13.7 0.7 convert_bitcast_fusion
  14.4 0.1 pad_maximum_fusion
  14.5 1.9 %collective-permute-start = (bf16[21,64,128]{2,0,1:T(8,128)(2,1)S(1)}, bf16[21,64,128]{2,0,1:T(8,128)(2,1)}, u32[]{:S(2)}, u32[]{:S(2)}) collective-permute-start(bf16[21,64,128]{2,0,1:T(8,128)(2,1)S(1)} %pad_maximum_fusion), channel_id=1, source_target_pairs={{0,4},{4,0},{8,12},{12,8},{16,20},{20,16},{24,28},{28,24},{32,36},... | collective-permute-start | bytes 1032200 | tf_op jit(solution)/shard_map/ppermute | solution.py:45
  16.4 3.8 %collective-permute-start.1 = (bf16[21,64,128]{2,0,1:T(8,128)(2,1)S(1)}, bf16[21,64,128]{2,0,1:T(8,128)(2,1)}, u32[]{:S(2)}, u32[]{:S(2)}) collective-permute-start(bf16[21,64,128]{2,0,1:T(8,128)(2,1)S(1)} %pad_maximum_fusion), channel_id=1, source_target_pairs={{0,32},{4,36},{8,40},{12,44},{16,48},{20,52},{24,56},{28,60},{32,0... | collective-permute-start | bytes 1032200 | tf_op jit(solution)/shard_map/ppermute | solution.py:45
  20.3 3.0 %reshape.52 = bf16[20,16,2,2048]{3,2,1,0:T(2,128)(2,1)} reshape(bf16[20,128,512]{2,1,0:T(8,128)(2,1)S(1)} %copy-done) | data formatting | bytes 5242880 | tf_op jit(solution)/shard_map/reshape | solution.py:71
  23.3 2.9 %copy.157 = bf16[16,20,2,2048]{3,0,2,1:T(8,128)(2,1)S(1)} copy(bf16[16,20,2,2048]{3,2,0,1:T(2,128)(2,1)} %bitcast.95) | data formatting | bytes 5242880 | tf_op jit(solution)/shard_map/transpose | solution.py:71
  26.2 8.2 %collective-permute-done.1 = bf16[21,64,128]{2,0,1:T(8,128)(2,1)} collective-permute-done((bf16[21,64,128]{2,0,1:T(8,128)(2,1)S(1)}, bf16[21,64,128]{2,0,1:T(8,128)(2,1)}, u32[]{:S(2)}, u32[]{:S(2)}) %collective-permute-start.1) | collective-permute-done | bytes 344096 | tf_op jit(solution)/shard_map/ppermute | solution.py:45
  34.3 2.9 %copy.162 = bf16[16,40,2048]{2,1,0:T(8,128)(2,1)} copy(bf16[16,40,2048]{2,0,1:T(8,128)(2,1)S(1)} %bitcast.94) | data formatting | bytes 5242880 | tf_op jit(solution)/shard_map/optimization_barrier | solution.py:74
  37.3 7.2 %all-to-all-start.1 = ((bf16[16,40,2048]{2,1,0:T(8,128)(2,1)}), bf16[16,40,2048]{2,1,0:T(8,128)(2,1)S(1)}, u32[]{:S(2)}, u32[]{:S(2)}) async-start(bf16[16,40,2048]{2,1,0:T(8,128)(2,1)} %copy.162), calls=%async_computation.1 | async-start | bytes 5242880 | tf_op jit(solution)/shard_map/all_to_all | solution.py:75
  44.5 1.9 %collective-permute-start.2 = (bf16[21,64,128]{2,0,1:T(8,128)(2,1)}, bf16[21,64,128]{2,0,1:T(8,128)(2,1)}, u32[]{:S(2)}, u32[]{:S(2)}) collective-permute-start(bf16[21,64,128]{2,0,1:T(8,128)(2,1)} %collective-permute-done.1), channel_id=1, source_target_pairs={{0,4},{4,0},{8,12},{12,8},{16,20},{20,16},{24,28},{28,24},{32,36},... | collective-permute-start | bytes 1032200 | tf_op jit(solution)/shard_map/ppermute | solution.py:45
  46.5 0.7 copy.156
  47.2 0.8 slice.82
  48.0 0.8 slice.81
  48.8 0.6 copy_bitcast_fusion.2
  49.4 2.1 %fusion.18 = bf16[84,32]{0,1:T(8,128)(2,1)S(1)} fusion(bf16[21,64,128]{2,0,1:T(8,128)(2,1)} %collective-permute-done.2, bf16[21,64,128]{2,0,1:T(8,128)(2,1)} %collective-permute-done.1, bf16[21,64,128]{2,0,1:T(8,128)(2,1)} %collective-permute-done, bf16[21,64,128]{2,0,1:T(8,128)(2,1)S(1)} %pad_maximum_fusion, bf16[32,64,128]{2,1,0:T(8,128)(2,1)S(1)} %all-to-all-done), kind=kOutput, calls=%fused_computation.19 | convolution fusion | flops 49547904 | bytes 1905920 | tf_op jit(solution)/shard_map/giq,wiq->gw/dot_general | solution.py:84
  51.5 0.1 fusion.26
  51.6 0.1 copy.161
  51.7 20.0 %all-gather.1 = bf16[4,148,128]{2,1,0:T(8,128)(2,1)S(1)} all-gather(bf16[1,148,128]{2,1,0:T(8,128)(2,1)S(1)} %copy.161), channel_id=2, replica_groups=mesh['chol'=128,'orb'=4] {'orb'}, dimensions={0}, use_global_device_ids=true | all-gather | bytes 189440 | tf_op jit(solution)/shard_map/all_gather | solution.py:86
  71.7 0.8 slice.101
  72.5 11.7 %all-to-all-done.1 = bf16[16,40,2048]{2,1,0:T(8,128)(2,1)S(1)} async-done(((bf16[16,40,2048]{2,1,0:T(8,128)(2,1)}), bf16[16,40,2048]{2,1,0:T(8,128)(2,1)S(1)}, u32[]{:S(2)}, u32[]{:S(2)}) %all-to-all-start.1) | async-done | bytes 2621472 | tf_op jit(solution)/shard_map/all_to_all | solution.py:75
  84.3 1.0 fusion.17
  85.3 0.1 reshape.59
  85.4 1.9 %collective-permute-start.6 = (bf16[640,2048]{1,0:T(8,128)(2,1)S(1)}, bf16[640,2048]{1,0:T(8,128)(2,1)}, u32[]{:S(2)}, u32[]{:S(2)}) collective-permute-start(bf16[640,2048]{1,0:T(8,128)(2,1)S(1)} %bitcast.92), channel_id=1, source_target_pairs={{0,4},{4,0},{8,12},{12,8},{16,20},{20,16},{24,28},{28,24},{32,36},... | collective-permute-start | bytes 7864328 | tf_op jit(solution)/shard_map/ppermute | solution.py:45
  87.5 0.1 copy.173
  87.6 0.1 copy.174
  87.8 0.1 pad_maximum_fusion.3
  87.9 0.1 copy.175
  88.0 0.1 broadcast_in_dim.25
  88.1 16.8 %all_to_all.20 = bf16[32,80,64]{1,2,0:T(8,128)(2,1)} all-to-all(bf16[32,80,64]{1,2,0:T(8,128)(2,1)S(1)} %bitcast.99), channel_id=1, replica_groups={{0,32,8,40,16,48,24,56,128,160,136,168,144,176,152,184,256,288,264,296,..., dimensions={0} | all-to-all | bytes 655360 | tf_op jit(solution)/shard_map/all_to_all | solution.py:103
  105.0 1.3 copy.176
  106.4 0.2 pad_maximum_fusion.1
  106.6 0.6 fusion.45
  107.2 2.4 %fusion = bf16[128,2048]{1,0:T(8,128)(2,1)S(1)} fusion(f32[128,2048]{1,0:T(8,128)S(1)} %fusion.45, bf16[640,128]{1,0:T(8,128)(2,1)S(1)} %bitcast.104, bf16[640,2048]{1,0:T(8,128)(2,1)} %collective-permute-done.6), kind=kOutput, calls=%fused_computation.1 | convolution fusion | flops 336068608 | bytes 4358144 | tf_op jit(solution)/shard_map/dot_general | solution.py:108
  109.6 0.5 copy.210
  110.1 0.9 reshape.63
  111.0 6.6 %all-to-all-start.3 = ((bf16[64,8,512]{2,1,0:T(8,128)(2,1)}), bf16[64,8,512]{2,1,0:T(8,128)(2,1)S(1)}, u32[]{:S(2)}, u32[]{:S(2)}) async-start(bf16[64,8,512]{2,1,0:T(8,128)(2,1)} %reshape.63), calls=%async_computation.3 | async-start | bytes 1048576 | tf_op jit(solution)/shard_map/all_to_all | solution.py:118
  117.6 0.1 reshape.55
  117.8 1.9 %collective-permute-start.3 = (f32[20,32]{0,1:T(8,128)S(1)}, f32[20,32]{0,1:T(8,128)S(1)}, u32[]{:S(2)}, u32[]{:S(2)}) collective-permute-start(f32[20,32]{0,1:T(8,128)S(1)} %bitcast.119), channel_id=1, source_target_pairs={{0,4},{4,0},{8,12},{12,8},{16,20},{20,16},{24,28},{28,24},{32,36},... | collective-permute-start | bytes 7688 | tf_op jit(solution)/shard_map/ppermute | solution.py:45
  119.7 3.6 %collective-permute-start.4 = (f32[20,32]{0,1:T(8,128)S(1)}, f32[20,32]{0,1:T(8,128)S(1)}, u32[]{:S(2)}, u32[]{:S(2)}) collective-permute-start(f32[20,32]{0,1:T(8,128)S(1)} %bitcast.117), channel_id=1, source_target_pairs={{0,32},{4,36},{8,40},{12,44},{16,48},{20,52},{24,56},{28,60},{32,0... | collective-permute-start | bytes 7688 | tf_op jit(solution)/shard_map/ppermute | solution.py:45
  123.3 2.1 %collective-permute-start.5 = (f32[20,32]{0,1:T(8,128)S(1)}, f32[20,32]{0,1:T(8,128)S(1)}, u32[]{:S(2)}, u32[]{:S(2)}) collective-permute-start(f32[20,32]{0,1:T(8,128)S(1)} %bitcast.115), channel_id=1, source_target_pairs={{0,36},{4,32},{8,44},{12,40},{16,52},{20,48},{24,60},{28,56},{32,4... | collective-permute-start | bytes 7688 | tf_op jit(solution)/shard_map/ppermute | solution.py:45
  125.4 3.0 %collective-permute-done.5 = f32[20,32]{0,1:T(8,128)S(1)} collective-permute-done((f32[20,32]{0,1:T(8,128)S(1)}, f32[20,32]{0,1:T(8,128)S(1)}, u32[]{:S(2)}, u32[]{:S(2)}) %collective-permute-start.5) | collective-permute-done | bytes 2592 | tf_op jit(solution)/shard_map/ppermute | solution.py:45
  128.6 0.7 copy.181
  129.3 5.6 %all-to-all-done.3 = bf16[64,8,512]{2,1,0:T(8,128)(2,1)S(1)} async-done(((bf16[64,8,512]{2,1,0:T(8,128)(2,1)}), bf16[64,8,512]{2,1,0:T(8,128)(2,1)S(1)}, u32[]{:S(2)}, u32[]{:S(2)}) %all-to-all-start.3) | async-done | bytes 524320 | tf_op jit(solution)/shard_map/all_to_all | solution.py:118
  135.1 0.2 fusion.12
  135.3 0.7 copy.182
  (40 shorter events, 0.7 us)
Async XLA Ops:
  0.6 19.7 %copy-start = (bf16[20,128,512]{2,1,0:T(8,128)(2,1)S(1)}, bf16[20,128,512]{2,1,0:T(8,128)(2,1)}, u32[]{:S(2)}) copy-start(bf16[20,128,512]{2,1,0:T(8,128)(2,1)} %param.8) | copy-start | bytes 7864324
  2.4 31.9 %all-to-all-start = ((bf16[32,64,128]{2,1,0:T(8,128)(2,1)}), bf16[32,64,128]{2,1,0:T(8,128)(2,1)S(1)}, u32[]{:S(2)}, u32[]{:S(2)}) async-start(bf16[32,64,128]{2,1,0:T(8,128)(2,1)} %broadcast_in_dim.22), calls=%async_computation | async-start | bytes 1048576 | tf_op jit(solution)/shard_map/all_to_all | solution.py:65
  14.5 11.6 %collective-permute-start = (bf16[21,64,128]{2,0,1:T(8,128)(2,1)S(1)}, bf16[21,64,128]{2,0,1:T(8,128)(2,1)}, u32[]{:S(2)}, u32[]{:S(2)}) collective-permute-start(bf16[21,64,128]{2,0,1:T(8,128)(2,1)S(1)} %pad_maximum_fusion), channel_id=1, source_target_pairs={{0,4},{4,0},{8,12},{12,8},{16,20},{20,16},{24,28},{28,24},{32,36},... | collective-permute-start | bytes 1032200 | tf_op jit(solution)/shard_map/ppermute | solution.py:45
  16.4 17.9 %collective-permute-start.1 = (bf16[21,64,128]{2,0,1:T(8,128)(2,1)S(1)}, bf16[21,64,128]{2,0,1:T(8,128)(2,1)}, u32[]{:S(2)}, u32[]{:S(2)}) collective-permute-start(bf16[21,64,128]{2,0,1:T(8,128)(2,1)S(1)} %pad_maximum_fusion), channel_id=1, source_target_pairs={{0,32},{4,36},{8,40},{12,44},{16,48},{20,52},{24,56},{28,60},{32,0... | collective-permute-start | bytes 1032200 | tf_op jit(solution)/shard_map/ppermute | solution.py:45
  37.3 9.2 %copy-start.4 = (bf16[1,64,128]{2,1,0:T(8,128)(2,1)S(1)}, bf16[1,64,128]{2,1,0:T(8,128)(2,1)}, u32[]{:S(2)}) copy-start(bf16[1,64,128]{2,1,0:T(8,128)(2,1)} %param.9) | copy-start | bytes 49156
  37.3 47.0 %all-to-all-start.1 = ((bf16[16,40,2048]{2,1,0:T(8,128)(2,1)}), bf16[16,40,2048]{2,1,0:T(8,128)(2,1)S(1)}, u32[]{:S(2)}, u32[]{:S(2)}) async-start(bf16[16,40,2048]{2,1,0:T(8,128)(2,1)} %copy.162), calls=%async_computation.1 | async-start | bytes 5242880 | tf_op jit(solution)/shard_map/all_to_all | solution.py:75
  44.5 4.9 %collective-permute-start.2 = (bf16[21,64,128]{2,0,1:T(8,128)(2,1)}, bf16[21,64,128]{2,0,1:T(8,128)(2,1)}, u32[]{:S(2)}, u32[]{:S(2)}) collective-permute-start(bf16[21,64,128]{2,0,1:T(8,128)(2,1)} %collective-permute-done.1), channel_id=1, source_target_pairs={{0,4},{4,0},{8,12},{12,8},{16,20},{20,16},{24,28},{28,24},{32,36},... | collective-permute-start | bytes 1032200 | tf_op jit(solution)/shard_map/ppermute | solution.py:45
  49.4 2.1 %copy-start.2 = (bf16[1,64,128]{1,2,0:T(8,128)(2,1)S(1)}, bf16[1,64,128]{1,2,0:T(8,128)(2,1)}, u32[]{:S(2)}) copy-start(bf16[1,64,128]{1,2,0:T(8,128)(2,1)} %copy.156) | copy-start | bytes 49156
  71.7 34.7 %copy-start.1 = (bf16[4,148,128]{2,1,0:T(8,128)(2,1)}, bf16[4,148,128]{2,1,0:T(8,128)(2,1)S(1)}, u32[]{:S(2)}) copy-start(bf16[4,148,128]{2,1,0:T(8,128)(2,1)S(1)} %all-gather.1) | copy-start | bytes 454660
  85.4 21.8 %collective-permute-start.6 = (bf16[640,2048]{1,0:T(8,128)(2,1)S(1)}, bf16[640,2048]{1,0:T(8,128)(2,1)}, u32[]{:S(2)}, u32[]{:S(2)}) collective-permute-start(bf16[640,2048]{1,0:T(8,128)(2,1)S(1)} %bitcast.92), channel_id=1, source_target_pairs={{0,4},{4,0},{8,12},{12,8},{16,20},{20,16},{24,28},{28,24},{32,36},... | collective-permute-start | bytes 7864328 | tf_op jit(solution)/shard_map/ppermute | solution.py:45
  109.5 25.5 %slice-start = ((bf16[4,148,128]{2,1,0:T(8,128)(2,1)}), bf16[4,64,128]{2,1,0:T(8,128)(2,1)S(1)}, s32[]{:S(2)}) async-start(bf16[4,148,128]{2,1,0:T(8,128)(2,1)} %copy-done.1), calls=%async_computation.4 | async-start | bytes 131072 | tf_op jit(solution)/shard_map/slice | solution.py:90
  109.6 25.5 %copy-start.3 = (bf16[1,64,128]{1,2,0:T(8,128)(2,1)S(1)}, bf16[1,64,128]{1,2,0:T(8,128)(2,1)}, u32[]{:S(2)}) copy-start(bf16[1,64,128]{1,2,0:T(8,128)(2,1)} %copy.156) | copy-start | bytes 49156
  111.0 23.9 %all-to-all-start.3 = ((bf16[64,8,512]{2,1,0:T(8,128)(2,1)}), bf16[64,8,512]{2,1,0:T(8,128)(2,1)S(1)}, u32[]{:S(2)}, u32[]{:S(2)}) async-start(bf16[64,8,512]{2,1,0:T(8,128)(2,1)} %reshape.63), calls=%async_computation.3 | async-start | bytes 1048576 | tf_op jit(solution)/shard_map/all_to_all | solution.py:118
  117.8 7.6 %collective-permute-start.3 = (f32[20,32]{0,1:T(8,128)S(1)}, f32[20,32]{0,1:T(8,128)S(1)}, u32[]{:S(2)}, u32[]{:S(2)}) collective-permute-start(f32[20,32]{0,1:T(8,128)S(1)} %bitcast.119), channel_id=1, source_target_pairs={{0,4},{4,0},{8,12},{12,8},{16,20},{20,16},{24,28},{28,24},{32,36},... | collective-permute-start | bytes 7688 | tf_op jit(solution)/shard_map/ppermute | solution.py:45
  119.7 5.7 %collective-permute-start.4 = (f32[20,32]{0,1:T(8,128)S(1)}, f32[20,32]{0,1:T(8,128)S(1)}, u32[]{:S(2)}, u32[]{:S(2)}) collective-permute-start(f32[20,32]{0,1:T(8,128)S(1)} %bitcast.117), channel_id=1, source_target_pairs={{0,32},{4,36},{8,40},{12,44},{16,48},{20,52},{24,56},{28,60},{32,0... | collective-permute-start | bytes 7688 | tf_op jit(solution)/shard_map/ppermute | solution.py:45
  123.3 5.1 %collective-permute-start.5 = (f32[20,32]{0,1:T(8,128)S(1)}, f32[20,32]{0,1:T(8,128)S(1)}, u32[]{:S(2)}, u32[]{:S(2)}) collective-permute-start(f32[20,32]{0,1:T(8,128)S(1)} %bitcast.115), channel_id=1, source_target_pairs={{0,36},{4,32},{8,44},{12,40},{16,52},{20,48},{24,60},{28,56},{32,4... | collective-permute-start | bytes 7688 | tf_op jit(solution)/shard_map/ppermute | solution.py:45

commit v4 on v3

--- a/solution.py
+++ b/solution.py
@@ -2,6 +2,7 @@
 import jax.numpy as jnp
 import numpy as np
 from jax import lax
+from jax.experimental.layout import Layout, with_layout_constraint
 from jax.sharding import PartitionSpec as P
 
 LEVEL_SCALE = 1.7320508
@@ -30,8 +31,8 @@
 Y, ZH, ZL, X, CORE = range(5)
 GREEN = groups_of((ZL, CORE), (Y, ZH, X))
 PLANE = groups_of((ZH, ZL, CORE), (Y, X))
-BLOCK = groups_of((ZH, CORE), (Y, X, ZL))
-HOME = groups_of((CORE,), (ZL, Y, ZH, X))
+BLOCK = groups_of((ZH, CORE), (Y, ZL, X))
+HOME = groups_of((CORE,), (Y, ZH, ZL, X))
 HOMES = len(HOME[0])
 CHIPS = len(PLANE[0])
 SHARES = np.zeros((MATES, len(PLACES), len(GREEN[0])), np.float32)
@@ -68,8 +69,8 @@
     sent = jnp.concatenate([rotated_chol, levels[None]], axis=0)
     held = [sent, to_mate(sent, 1), to_mate(sent, 2)]
 
-    chol_rows = chol_vectors.reshape(own, CHIPS, 2, rows // 2 * basis).transpose(1, 0, 2, 3)
-    chol_rows = chol_rows.reshape(CHIPS, own * 2, rows // 2 * basis)
+    chol_rows = chol_vectors.reshape(own * 2, CHIPS, rows // 2 * basis).transpose(1, 0, 2)
+    chol_rows = with_layout_constraint(chol_rows, Layout((0, 1, 2)))
 
     green, chol_rows, held = lax.optimization_barrier((green, chol_rows, held))
     chol_mine = lax.all_to_all(chol_rows, "chol", 0, 0, axis_index_groups=PLANE)
@@ -98,11 +99,12 @@
         [jnp.concatenate([aux_field, zero], axis=3), jnp.concatenate([zero, aux_field], axis=3)],
         axis=3,
     ).reshape(2, 2 * own * 2, 2 * share)
-    aux_sent = jnp.broadcast_to(aux_field[None], (CHIPS,) + aux_field.shape)
+    aux_sent = jnp.broadcast_to(aux_field[None, :, None], (SIDE, 2, SIDE) + aux_field.shape[1:])
     aux_sent = aux_sent.reshape((CHIPS * 2,) + aux_field.shape[1:])
     aux_all = lax.all_to_all(aux_sent, "chol", 0, 0, axis_index_groups=BLOCK)
-    aux_all = aux_all.reshape(CHIPS, 2, 2, own * 2, 2 * share)
-    aux_all = jnp.concatenate([aux_all[:, 0], aux_all[:, 1]], axis=3)
+    aux_all = aux_all.reshape(SIDE, 2, SIDE, 2, own * 2, 2 * share)
+    aux_all = jnp.concatenate([aux_all[:, 0], aux_all[:, 1]], axis=4)
+    aux_all = aux_all.reshape(CHIPS, 2, own * 2, 4 * share)
     chol_others = to_mate(chol_mine, 1)
     potential = sum(
         lax.dot_general(
@@ -113,11 +115,12 @@
         )
         for i, part in enumerate((chol_mine, chol_others))
     )
-    potential = potential.astype(bf16).reshape(2, 2, share, rows // 2 * basis)
-    potential = potential.transpose(0, 2, 1, 3).reshape(HOMES, rows, basis)
+    potential = potential.astype(bf16).reshape(2, 2, SIDE * 2, SIDE, rows // 2 * basis)
+    potential = potential.transpose(2, 0, 3, 1, 4).reshape(HOMES, rows, basis)
     parts = lax.all_to_all(potential, "chol", 0, 0, axis_index_groups=HOME)
-    parts = parts.reshape(2, SIDE, 2, SIDE, rows, basis)
-    total = jnp.sum(parts.astype(f32), axis=(0, 2)).astype(bf16)
+    parts = parts.reshape(SIDE, SIDE, SIDE, rows, basis)
+    total = jnp.sum(parts.astype(f32), axis=1).astype(bf16)
+    total = total.reshape(CHIPS, 2, rows // 2, basis).transpose(1, 0, 2, 3)
 
     applied = jnp.einsum(
         "biq,pbq->ip",

time: 137 us -> 135 us (0.985)
  the two profiles are of different devices: /device:TPU:128 before, /device:TPU:1 now
where the time goes in v4:
time: 135 us; the launch traced here: 133 us
  starting transfers between devices  46.9 us (35%)
  blocking collectives  37.7 us (28%)
  waiting for transfers between devices  20.8 us (15%)
  local copies, waits for them, and re-layouts  19.3 us (14%)
  matrix products  6.15 us (5%)
  other arithmetic  1.43 us (1%)
    all_gather x1, blocking collectives, shards(): lax.all_gather(jnp.concatenate([walkers[0], partial_bias], axis=0), 'orb'...  23.3 us
    ppermute x7, starting transfers between devices, to_mate(): lax.ppermute(array, 'chol', [(i, i ^ step) for i in range(len(PLACES))])  21.5 us
    all_to_all x1, blocking collectives, shards(): aux_all = lax.all_to_all(aux_sent, 'chol', 0, 0, axis_index_groups=BLOCK)  14.4 us
    all_to_all x1, starting transfers between devices, shards(): green = lax.all_to_all(green, 'chol', 0, 0, axis_index_groups=GREEN)  10.6 us
    all_to_all x1, starting transfers between devices, shards(): parts = lax.all_to_all(potential, 'chol', 0, 0, axis_index_groups=HOME)  7.84 us
    ppermute x7, waiting for transfers between devices, to_mate(): lax.ppermute(array, 'chol', [(i, i ^ step) for i in range(len(PLACES))])  7.72 us
    reshape x2, local copies, waits for them, and re-layouts, shards(): chol_vectors.reshape(own * 2, CHIPS, rows // 2 * basis).transpose(1, 0, 2)  7.04 us
    all_to_all x1, starting transfers between devices, shards(): chol_mine = lax.all_to_all(chol_rows, 'chol', 0, 0, axis_index_groups=PLANE)  6.94 us
  transfers between devices with their start and end apart: 10, of which 4 were waited for; matrix products, arithmetic and copies ran while one was open for 14% of the time, Pallas kernels for 0%

profile of v4, /device:TPU:1, one launch (start us, length us, event | category | flops | bytes accessed | tf_op | source)
XLA Modules:
  0.0 133.4 jit_solution(18395947048312689838)
XLA Ops:
  0.6 1.6 %broadcast_in_dim.22 = bf16[32,64,128]{2,1,0:T(8,128)(2,1)} broadcast(bf16[64,128]{1,0:T(8,128)(2,1)} %bitcast.116), dimensions={1,2} | broadcast | bytes 540672 | tf_op jit(solution)/shard_map/broadcast_in_dim | solution.py:65
  2.3 10.6 %all-to-all-start = ((bf16[32,64,128]{2,1,0:T(8,128)(2,1)}), bf16[32,64,128]{2,1,0:T(8,128)(2,1)S(1)}, u32[]{:S(2)}, u32[]{:S(2)}) async-start(bf16[32,64,128]{2,1,0:T(8,128)(2,1)} %broadcast_in_dim.22), calls=%async_computation | async-start | bytes 1048576 | tf_op jit(solution)/shard_map/all_to_all | solution.py:66
  12.8 1.2 copy.154
  14.0 0.7 convert_bitcast_fusion
  14.8 0.1 pad_maximum_fusion
  14.9 2.9 %collective-permute-start = (bf16[21,64,128]{2,0,1:T(8,128)(2,1)S(1)}, bf16[21,64,128]{2,0,1:T(8,128)(2,1)}, u32[]{:S(2)}, u32[]{:S(2)}) collective-permute-start(bf16[21,64,128]{2,0,1:T(8,128)(2,1)S(1)} %pad_maximum_fusion), channel_id=1, source_target_pairs={{0,4},{4,0},{8,12},{12,8},{16,20},{20,16},{24,28},{28,24},{32,36},... | collective-permute-start | bytes 1032200 | tf_op jit(solution)/shard_map/ppermute | solution.py:46
  17.8 3.5 %collective-permute-start.1 = (bf16[21,64,128]{2,0,1:T(8,128)(2,1)S(1)}, bf16[21,64,128]{2,0,1:T(8,128)(2,1)}, u32[]{:S(2)}, u32[]{:S(2)}) collective-permute-start(bf16[21,64,128]{2,0,1:T(8,128)(2,1)S(1)} %pad_maximum_fusion), channel_id=1, source_target_pairs={{0,32},{4,36},{8,40},{12,44},{16,48},{20,52},{24,56},{28,60},{32,0... | collective-permute-start | bytes 1032200 | tf_op jit(solution)/shard_map/ppermute | solution.py:46
  21.3 4.1 %reshape.57 = bf16[40,16,2048]{2,1,0:T(8,128)(2,1)S(1)} reshape(bf16[20,128,512]{2,1,0:T(8,128)(2,1)} %param.8) | data formatting | bytes 5242880 | tf_op jit(solution)/shard_map/reshape | solution.py:72
  25.4 2.9 %copy.210 = bf16[40,16,2048]{2,0,1:T(8,128)(2,1)} copy(bf16[40,16,2048]{2,1,0:T(8,128)(2,1)S(1)} %reshape.57) | data formatting | bytes 5242880 | tf_op jit(solution)/shard_map/reshape | solution.py:72
  28.4 6.6 %collective-permute-done.1 = bf16[21,64,128]{2,0,1:T(8,128)(2,1)} collective-permute-done((bf16[21,64,128]{2,0,1:T(8,128)(2,1)S(1)}, bf16[21,64,128]{2,0,1:T(8,128)(2,1)}, u32[]{:S(2)}, u32[]{:S(2)}) %collective-permute-start.1) | collective-permute-done | bytes 344096 | tf_op jit(solution)/shard_map/ppermute | solution.py:46
  35.0 6.9 %all-to-all-start.1 = ((bf16[16,40,2048]{2,1,0:T(8,128)(2,1)}), bf16[16,40,2048]{2,1,0:T(8,128)(2,1)S(1)}, u32[]{:S(2)}, u32[]{:S(2)}) async-start(bf16[16,40,2048]{2,1,0:T(8,128)(2,1)} %bitcast.95), calls=%async_computation.1 | async-start | bytes 5242880 | tf_op jit(solution)/shard_map/all_to_all | solution.py:76
  41.9 2.9 %collective-permute-start.2 = (bf16[21,64,128]{2,0,1:T(8,128)(2,1)}, bf16[21,64,128]{2,0,1:T(8,128)(2,1)}, u32[]{:S(2)}, u32[]{:S(2)}) collective-permute-start(bf16[21,64,128]{2,0,1:T(8,128)(2,1)} %collective-permute-done.1), channel_id=1, source_target_pairs={{0,4},{4,0},{8,12},{12,8},{16,20},{20,16},{24,28},{28,24},{32,36},... | collective-permute-start | bytes 1032200 | tf_op jit(solution)/shard_map/ppermute | solution.py:46
  44.9 0.7 copy.152
  45.6 0.8 slice.82
  46.4 0.8 slice.81
  47.2 0.6 copy_bitcast_fusion.3
  47.8 2.1 %fusion.18 = bf16[84,32]{0,1:T(8,128)(2,1)S(1)} fusion(bf16[21,64,128]{2,0,1:T(8,128)(2,1)} %collective-permute-done.2, bf16[21,64,128]{2,0,1:T(8,128)(2,1)} %collective-permute-done.1, bf16[21,64,128]{2,0,1:T(8,128)(2,1)} %collective-permute-done, bf16[21,64,128]{2,0,1:T(8,128)(2,1)S(1)} %pad_maximum_fusion, bf16[32,64,128]{2,1,0:T(8,128)(2,1)S(1)} %all-to-all-done), kind=kOutput, calls=%fused_computation.20 | convolution fusion | flops 49547904 | bytes 1905920 | tf_op jit(solution)/shard_map/giq,wiq->gw/dot_general | solution.py:85
  49.9 0.1 fusion.26
  50.0 0.1 copy.157
  50.1 23.3 %all-gather.1 = bf16[4,148,128]{2,1,0:T(8,128)(2,1)S(1)} all-gather(bf16[1,148,128]{2,1,0:T(8,128)(2,1)S(1)} %copy.157), channel_id=2, replica_groups=mesh['chol'=128,'orb'=4] {'orb'}, dimensions={0}, use_global_device_ids=true | all-gather | bytes 189440 | tf_op jit(solution)/shard_map/all_gather | solution.py:87
  73.4 0.8 slice.101
  74.2 6.6 %all-to-all-done.1 = bf16[16,40,2048]{2,1,0:T(8,128)(2,1)S(1)} async-done(((bf16[16,40,2048]{2,1,0:T(8,128)(2,1)}), bf16[16,40,2048]{2,1,0:T(8,128)(2,1)S(1)}, u32[]{:S(2)}, u32[]{:S(2)}) %all-to-all-start.1) | async-done | bytes 2621472 | tf_op jit(solution)/shard_map/all_to_all | solution.py:76
  80.9 1.0 fusion.17
  81.9 0.1 reshape.63
  81.9 3.7 %collective-permute-start.6 = (bf16[640,2048]{1,0:T(8,128)(2,1)S(1)}, bf16[640,2048]{1,0:T(8,128)(2,1)}, u32[]{:S(2)}, u32[]{:S(2)}) collective-permute-start(bf16[640,2048]{1,0:T(8,128)(2,1)S(1)} %bitcast.93), channel_id=1, source_target_pairs={{0,4},{4,0},{8,12},{12,8},{16,20},{20,16},{24,28},{28,24},{32,36},... | collective-permute-start | bytes 7864328 | tf_op jit(solution)/shard_map/ppermute | solution.py:46
  85.9 0.1 copy.168
  86.0 0.1 copy.169
  86.2 0.1 pad_maximum_fusion.3
  86.3 0.1 copy.170
  86.4 0.1 broadcast_in_dim.25
  86.5 14.4 %all_to_all.20 = bf16[32,80,64]{1,2,0:T(8,128)(2,1)} all-to-all(bf16[32,80,64]{1,2,0:T(8,128)(2,1)S(1)} %bitcast.98), channel_id=1, replica_groups={{0,8,16,24,32,40,48,56,128,136,144,152,160,168,176,184,256,264,272,280,..., dimensions={0} | all-to-all | bytes 655360 | tf_op jit(solution)/shard_map/all_to_all | solution.py:104
  100.9 1.3 %copy.171 = bf16[32,80,64]{2,1,0:T(8,128)(2,1)S(1)} copy(bf16[32,80,64]{1,2,0:T(8,128)(2,1)} %all_to_all.20) | data formatting | bytes 655360 | tf_op jit(solution)/shard_map/all_to_all | solution.py:104
  102.3 0.2 pad_maximum_fusion.1
  102.5 0.6 fusion.46
  103.1 2.3 %fusion = bf16[128,2048]{1,0:T(8,128)(2,1)S(1)} fusion(f32[128,2048]{1,0:T(8,128)S(1)} %fusion.46, bf16[640,128]{1,0:T(8,128)(2,1)S(1)} %bitcast.105, bf16[640,2048]{1,0:T(8,128)(2,1)} %collective-permute-done.6), kind=kOutput, calls=%fused_computation.2 | convolution fusion | flops 336068608 | bytes 4358144 | tf_op jit(solution)/shard_map/dot_general | solution.py:110
  105.5 0.2 reshape.66
  105.7 0.5 copy.211
  106.3 0.9 reshape.67
  107.2 7.8 %all-to-all-start.3 = ((bf16[64,8,512]{2,1,0:T(8,128)(2,1)}), bf16[64,8,512]{2,1,0:T(8,128)(2,1)S(1)}, u32[]{:S(2)}, u32[]{:S(2)}) async-start(bf16[64,8,512]{2,1,0:T(8,128)(2,1)} %reshape.67), calls=%async_computation.3 | async-start | bytes 1048576 | tf_op jit(solution)/shard_map/all_to_all | solution.py:120
  115.0 0.1 reshape.59
  115.2 2.9 %collective-permute-start.4 = (f32[20,32]{0,1:T(8,128)S(1)}, f32[20,32]{0,1:T(8,128)S(1)}, u32[]{:S(2)}, u32[]{:S(2)}) collective-permute-start(f32[20,32]{0,1:T(8,128)S(1)} %bitcast.121), channel_id=1, source_target_pairs={{0,32},{4,36},{8,40},{12,44},{16,48},{20,52},{24,56},{28,60},{32,0... | collective-permute-start | bytes 7688 | tf_op jit(solution)/shard_map/ppermute | solution.py:46
  118.1 3.7 %collective-permute-start.5 = (f32[20,32]{0,1:T(8,128)S(1)}, f32[20,32]{0,1:T(8,128)S(1)}, u32[]{:S(2)}, u32[]{:S(2)}) collective-permute-start(f32[20,32]{0,1:T(8,128)S(1)} %bitcast.119), channel_id=1, source_target_pairs={{0,36},{4,32},{8,44},{12,40},{16,52},{20,48},{24,60},{28,56},{32,4... | collective-permute-start | bytes 7688 | tf_op jit(solution)/shard_map/ppermute | solution.py:46
  121.8 1.9 %collective-permute-start.3 = (f32[20,32]{0,1:T(8,128)S(1)}, f32[20,32]{0,1:T(8,128)S(1)}, u32[]{:S(2)}, u32[]{:S(2)}) collective-permute-start(f32[20,32]{0,1:T(8,128)S(1)} %bitcast.117), channel_id=1, source_target_pairs={{0,4},{4,0},{8,12},{12,8},{16,20},{20,16},{24,28},{28,24},{32,36},... | collective-permute-start | bytes 7688 | tf_op jit(solution)/shard_map/ppermute | solution.py:46
  123.8 1.1 collective-permute-done.3
  125.1 0.7 copy.178
  125.8 6.5 %all-to-all-done.3 = bf16[64,8,512]{2,1,0:T(8,128)(2,1)S(1)} async-done(((bf16[64,8,512]{2,1,0:T(8,128)(2,1)}), bf16[64,8,512]{2,1,0:T(8,128)(2,1)S(1)}, u32[]{:S(2)}, u32[]{:S(2)}) %all-to-all-start.3) | async-done | bytes 524320 | tf_op jit(solution)/shard_map/all_to_all | solution.py:120
  132.5 0.2 fusion.12
  132.7 0.7 copy.179
  (40 shorter events, 0.8 us)
Async XLA Ops:
  2.3 32.7 %all-to-all-start = ((bf16[32,64,128]{2,1,0:T(8,128)(2,1)}), bf16[32,64,128]{2,1,0:T(8,128)(2,1)S(1)}, u32[]{:S(2)}, u32[]{:S(2)}) async-start(bf16[32,64,128]{2,1,0:T(8,128)(2,1)} %broadcast_in_dim.22), calls=%async_computation | async-start | bytes 1048576 | tf_op jit(solution)/shard_map/all_to_all | solution.py:66
  14.9 13.5 %collective-permute-start = (bf16[21,64,128]{2,0,1:T(8,128)(2,1)S(1)}, bf16[21,64,128]{2,0,1:T(8,128)(2,1)}, u32[]{:S(2)}, u32[]{:S(2)}) collective-permute-start(bf16[21,64,128]{2,0,1:T(8,128)(2,1)S(1)} %pad_maximum_fusion), channel_id=1, source_target_pairs={{0,4},{4,0},{8,12},{12,8},{16,20},{20,16},{24,28},{28,24},{32,36},... | collective-permute-start | bytes 1032200 | tf_op jit(solution)/shard_map/ppermute | solution.py:46
  17.8 17.2 %collective-permute-start.1 = (bf16[21,64,128]{2,0,1:T(8,128)(2,1)S(1)}, bf16[21,64,128]{2,0,1:T(8,128)(2,1)}, u32[]{:S(2)}, u32[]{:S(2)}) collective-permute-start(bf16[21,64,128]{2,0,1:T(8,128)(2,1)S(1)} %pad_maximum_fusion), channel_id=1, source_target_pairs={{0,32},{4,36},{8,40},{12,44},{16,48},{20,52},{24,56},{28,60},{32,0... | collective-permute-start | bytes 1032200 | tf_op jit(solution)/shard_map/ppermute | solution.py:46
  35.0 9.9 %copy-start.3 = (bf16[1,64,128]{2,1,0:T(8,128)(2,1)S(1)}, bf16[1,64,128]{2,1,0:T(8,128)(2,1)}, u32[]{:S(2)}) copy-start(bf16[1,64,128]{2,1,0:T(8,128)(2,1)} %param.9) | copy-start | bytes 49156
  35.0 45.8 %all-to-all-start.1 = ((bf16[16,40,2048]{2,1,0:T(8,128)(2,1)}), bf16[16,40,2048]{2,1,0:T(8,128)(2,1)S(1)}, u32[]{:S(2)}, u32[]{:S(2)}) async-start(bf16[16,40,2048]{2,1,0:T(8,128)(2,1)} %bitcast.95), calls=%async_computation.1 | async-start | bytes 5242880 | tf_op jit(solution)/shard_map/all_to_all | solution.py:76
  41.9 5.9 %collective-permute-start.2 = (bf16[21,64,128]{2,0,1:T(8,128)(2,1)}, bf16[21,64,128]{2,0,1:T(8,128)(2,1)}, u32[]{:S(2)}, u32[]{:S(2)}) collective-permute-start(bf16[21,64,128]{2,0,1:T(8,128)(2,1)} %collective-permute-done.1), channel_id=1, source_target_pairs={{0,4},{4,0},{8,12},{12,8},{16,20},{20,16},{24,28},{28,24},{32,36},... | collective-permute-start | bytes 1032200 | tf_op jit(solution)/shard_map/ppermute | solution.py:46
  47.8 2.1 %copy-start.1 = (bf16[1,64,128]{1,2,0:T(8,128)(2,1)S(1)}, bf16[1,64,128]{1,2,0:T(8,128)(2,1)}, u32[]{:S(2)}) copy-start(bf16[1,64,128]{1,2,0:T(8,128)(2,1)} %copy.152) | copy-start | bytes 49156
  73.4 29.0 %copy-start = (bf16[4,148,128]{2,1,0:T(8,128)(2,1)}, bf16[4,148,128]{2,1,0:T(8,128)(2,1)S(1)}, u32[]{:S(2)}) copy-start(bf16[4,148,128]{2,1,0:T(8,128)(2,1)S(1)} %all-gather.1) | copy-start | bytes 454660
  81.9 21.2 %collective-permute-start.6 = (bf16[640,2048]{1,0:T(8,128)(2,1)S(1)}, bf16[640,2048]{1,0:T(8,128)(2,1)}, u32[]{:S(2)}, u32[]{:S(2)}) collective-permute-start(bf16[640,2048]{1,0:T(8,128)(2,1)S(1)} %bitcast.93), channel_id=1, source_target_pairs={{0,4},{4,0},{8,12},{12,8},{16,20},{20,16},{24,28},{28,24},{32,36},... | collective-permute-start | bytes 7864328 | tf_op jit(solution)/shard_map/ppermute | solution.py:46
  106.2 26.3 %slice-start = ((bf16[4,148,128]{2,1,0:T(8,128)(2,1)}), bf16[4,64,128]{2,1,0:T(8,128)(2,1)S(1)}, s32[]{:S(2)}) async-start(bf16[4,148,128]{2,1,0:T(8,128)(2,1)} %copy-done), calls=%async_computation.4 | async-start | bytes 131072 | tf_op jit(solution)/shard_map/slice | solution.py:91
  106.3 26.3 %copy-start.2 = (bf16[1,64,128]{1,2,0:T(8,128)(2,1)S(1)}, bf16[1,64,128]{1,2,0:T(8,128)(2,1)}, u32[]{:S(2)}) copy-start(bf16[1,64,128]{1,2,0:T(8,128)(2,1)} %copy.152) | copy-start | bytes 49156
  107.2 25.1 %all-to-all-start.3 = ((bf16[64,8,512]{2,1,0:T(8,128)(2,1)}), bf16[64,8,512]{2,1,0:T(8,128)(2,1)S(1)}, u32[]{:S(2)}, u32[]{:S(2)}) async-start(bf16[64,8,512]{2,1,0:T(8,128)(2,1)} %reshape.67), calls=%async_computation.3 | async-start | bytes 1048576 | tf_op jit(solution)/shard_map/all_to_all | solution.py:120
  115.2 8.5 %collective-permute-start.4 = (f32[20,32]{0,1:T(8,128)S(1)}, f32[20,32]{0,1:T(8,128)S(1)}, u32[]{:S(2)}, u32[]{:S(2)}) collective-permute-start(f32[20,32]{0,1:T(8,128)S(1)} %bitcast.121), channel_id=1, source_target_pairs={{0,32},{4,36},{8,40},{12,44},{16,48},{20,52},{24,56},{28,60},{32,0... | collective-permute-start | bytes 7688 | tf_op jit(solution)/shard_map/ppermute | solution.py:46
  118.1 5.6 %collective-permute-start.5 = (f32[20,32]{0,1:T(8,128)S(1)}, f32[20,32]{0,1:T(8,128)S(1)}, u32[]{:S(2)}, u32[]{:S(2)}) collective-permute-start(f32[20,32]{0,1:T(8,128)S(1)} %bitcast.119), channel_id=1, source_target_pairs={{0,36},{4,32},{8,44},{12,40},{16,52},{20,48},{24,60},{28,56},{32,4... | collective-permute-start | bytes 7688 | tf_op jit(solution)/shard_map/ppermute | solution.py:46
  121.8 3.1 %collective-permute-start.3 = (f32[20,32]{0,1:T(8,128)S(1)}, f32[20,32]{0,1:T(8,128)S(1)}, u32[]{:S(2)}, u32[]{:S(2)}) collective-permute-start(f32[20,32]{0,1:T(8,128)S(1)} %bitcast.117), channel_id=1, source_target_pairs={{0,4},{4,0},{8,12},{12,8},{16,20},{20,16},{24,28},{28,24},{32,36},... | collective-permute-start | bytes 7688 | tf_op jit(solution)/shard_map/ppermute | solution.py:46

commit v5 on v4

--- a/solution.py
+++ b/solution.py
@@ -31,7 +31,8 @@
 Y, ZH, ZL, X, CORE = range(5)
 GREEN = groups_of((ZL, CORE), (Y, ZH, X))
 PLANE = groups_of((ZH, ZL, CORE), (Y, X))
-BLOCK = groups_of((ZH, CORE), (Y, ZL, X))
+LINE = groups_of((Y, ZH, ZL, CORE), (X,))
+BLOCK = groups_of((ZH, X, CORE), (Y, ZL))
 HOME = groups_of((CORE,), (Y, ZH, ZL, X))
 HOMES = len(HOME[0])
 CHIPS = len(PLANE[0])
@@ -83,14 +84,16 @@
 
     rotated = jnp.concatenate(held, axis=0)
     partial_bias = jnp.einsum("giq,wiq->gw", rotated, green, preferred_element_type=f32)
-    partial_bias = jnp.pad(partial_bias.astype(bf16), ((0, 0), (0, width - share)))
+    upper = lax.reduce_precision(partial_bias, 8, 7)
+    partial_bias = jnp.concatenate([upper, partial_bias - upper], axis=1).astype(bf16)
+    partial_bias = jnp.pad(partial_bias, ((0, 0), (0, width - 2 * share)))
+    partial_bias, levels = lax.optimization_barrier((partial_bias, levels))
     gathered = lax.all_gather(
         jnp.concatenate([walkers[0], partial_bias], axis=0), "orb", axis=0, tiled=False
     )
-    bias = jnp.sum(gathered[:, occupied:, :share].astype(f32), axis=0)
+    bias = jnp.sum(gathered[:, occupied:, : 2 * share].astype(f32), axis=0)
+    bias = bias[:, :share] + bias[:, share:]
     walker_full = gathered[:, :occupied]
-    bias, chol_mine, walker_full = lax.optimization_barrier((bias, chol_mine, walker_full))
-
     aux_field = (LEVEL_SCALE * levels - TAU_ROOT * bias).astype(bf16)
     aux_field = aux_field.reshape(2, 2, own + 1, share)[:, :, :own]
     aux_field = jnp.where(zl == 0, aux_field, jnp.stack([aux_field[1], aux_field[0]]))
@@ -99,8 +102,10 @@
         [jnp.concatenate([aux_field, zero], axis=3), jnp.concatenate([zero, aux_field], axis=3)],
         axis=3,
     ).reshape(2, 2 * own * 2, 2 * share)
-    aux_sent = jnp.broadcast_to(aux_field[None, :, None], (SIDE, 2, SIDE) + aux_field.shape[1:])
-    aux_sent = aux_sent.reshape((CHIPS * 2,) + aux_field.shape[1:])
+    aux_field = lax.all_gather(aux_field, "chol", axis=1, axis_index_groups=LINE, tiled=False)
+    aux_field, chol_mine, bias = lax.optimization_barrier((aux_field, chol_mine, bias))
+    aux_sent = jnp.broadcast_to(aux_field[None], (SIDE,) + aux_field.shape)
+    aux_sent = aux_sent.reshape(SIDE * 2, SIDE * 2 * own * 2, 2 * share)
     aux_all = lax.all_to_all(aux_sent, "chol", 0, 0, axis_index_groups=BLOCK)
     aux_all = aux_all.reshape(SIDE, 2, SIDE, 2, own * 2, 2 * share)
     aux_all = jnp.concatenate([aux_all[:, 0], aux_all[:, 1]], axis=4)

time: 135 us -> 138 us (1.022)
  blocking collectives: 37.7 us -> 45.5 us
  waiting for transfers between devices: 20.8 us -> 14.3 us
    all_gather x0 -> x1, blocking collectives: none -> 9.94 us  [shards(): lax.all_gather(aux_field, 'chol', axis=1, axis_index_groups=LINE, tiled=F...]
    all_to_all x1, waiting for transfers between devices: 6.59 us -> 0.01 us  [shards(): chol_mine = lax.all_to_all(chol_rows, 'chol', 0, 0, axis_index_groups=PLANE)]
    ppermute x7, starting transfers between devices: 21.5 us -> 24.3 us  [to_mate(): lax.ppermute(array, 'chol', [(i, i ^ step) for i in range(len(PLACES))])]
    all_to_all x1, blocking collectives: 14.4 us -> 12.3 us  [shards(): aux_all = lax.all_to_all(aux_sent, 'chol', 0, 0, axis_index_groups=BLOCK)]
    all_to_all x1, starting transfers between devices: 7.84 us -> 6.19 us  [shards(): parts = lax.all_to_all(potential, 'chol', 0, 0, axis_index_groups=HOME)]
    unnamed x18 -> x20, local copies, waits for them, and re-layouts: 4.02 us -> 4.15 us
  transfers between devices with their start and end apart: 10 -> 10, of which waited for: 4 -> 4; matrix products, arithmetic and copies ran while one was open for 14% -> 15% of each run, Pallas kernels for 0% -> 0%
where the time goes in v5:
time: 138 us; the launch traced here: 137 us
  starting transfers between devices  48 us (35%)
  blocking collectives  45.5 us (33%)
  local copies, waits for them, and re-layouts  19.9 us (14%)
  waiting for transfers between devices  14.3 us (10%)
  matrix products  6.98 us (5%)
  other arithmetic  1.47 us (1%)
    ppermute x7, starting transfers between devices, to_mate(): lax.ppermute(array, 'chol', [(i, i ^ step) for i in range(len(PLACES))])  24.3 us
    all_gather x1, blocking collectives, shards(): lax.all_gather(jnp.concatenate([walkers[0], partial_bias], axis=0), 'orb'...  23.3 us
    all_to_all x1, blocking collectives, shards(): aux_all = lax.all_to_all(aux_sent, 'chol', 0, 0, axis_index_groups=BLOCK)  12.3 us
    all_to_all x1, starting transfers between devices, shards(): green = lax.all_to_all(green, 'chol', 0, 0, axis_index_groups=GREEN)  10.6 us
    all_gather x1, blocking collectives, shards(): lax.all_gather(aux_field, 'chol', axis=1, axis_index_groups=LINE, tiled=F...  9.94 us
    ppermute x7, waiting for transfers between devices, to_mate(): lax.ppermute(array, 'chol', [(i, i ^ step) for i in range(len(PLACES))])  7.51 us
    reshape x2, local copies, waits for them, and re-layouts, shards(): chol_vectors.reshape(own * 2, CHIPS, rows // 2 * basis).transpose(1, 0, 2)  7.04 us
    all_to_all x1, starting transfers between devices, shards(): chol_mine = lax.all_to_all(chol_rows, 'chol', 0, 0, axis_index_groups=PLANE)  6.94 us
  transfers between devices with their start and end apart: 10, of which 4 were waited for; matrix products, arithmetic and copies ran while one was open for 15% of the time, Pallas kernels for 0%

profile of v5, /device:TPU:1, one launch (start us, length us, event | category | flops | bytes accessed | tf_op | source)
XLA Modules:
  0.0 137.3 jit_solution(5943448604745247378)
XLA Ops:
  0.6 1.6 %broadcast_in_dim.21 = bf16[32,64,128]{2,1,0:T(8,128)(2,1)} broadcast(bf16[64,128]{1,0:T(8,128)(2,1)} %bitcast.109), dimensions={1,2} | broadcast | bytes 540672 | tf_op jit(solution)/shard_map/broadcast_in_dim | solution.py:66
  2.3 10.6 %all-to-all-start = ((bf16[32,64,128]{2,1,0:T(8,128)(2,1)}), bf16[32,64,128]{2,1,0:T(8,128)(2,1)S(1)}, u32[]{:S(2)}, u32[]{:S(2)}) async-start(bf16[32,64,128]{2,1,0:T(8,128)(2,1)} %broadcast_in_dim.21), calls=%async_computation | async-start | bytes 1048576 | tf_op jit(solution)/shard_map/all_to_all | solution.py:67
  12.8 0.7 convert_bitcast_fusion
  13.6 1.2 copy.157
  14.8 0.1 pad_maximum_fusion
  14.9 2.9 %collective-permute-start = (bf16[21,64,128]{2,0,1:T(8,128)(2,1)S(1)}, bf16[21,64,128]{2,0,1:T(8,128)(2,1)}, u32[]{:S(2)}, u32[]{:S(2)}) collective-permute-start(bf16[21,64,128]{2,0,1:T(8,128)(2,1)S(1)} %pad_maximum_fusion), channel_id=1, source_target_pairs={{0,4},{4,0},{8,12},{12,8},{16,20},{20,16},{24,28},{28,24},{32,36},... | collective-permute-start | bytes 1032200 | tf_op jit(solution)/shard_map/ppermute | solution.py:47
  17.8 3.5 %collective-permute-start.1 = (bf16[21,64,128]{2,0,1:T(8,128)(2,1)S(1)}, bf16[21,64,128]{2,0,1:T(8,128)(2,1)}, u32[]{:S(2)}, u32[]{:S(2)}) collective-permute-start(bf16[21,64,128]{2,0,1:T(8,128)(2,1)S(1)} %pad_maximum_fusion), channel_id=1, source_target_pairs={{0,32},{4,36},{8,40},{12,44},{16,48},{20,52},{24,56},{28,60},{32,0... | collective-permute-start | bytes 1032200 | tf_op jit(solution)/shard_map/ppermute | solution.py:47
  21.3 4.1 %reshape.57 = bf16[40,16,2048]{2,1,0:T(8,128)(2,1)S(1)} reshape(bf16[20,128,512]{2,1,0:T(8,128)(2,1)} %param.8) | data formatting | bytes 5242880 | tf_op jit(solution)/shard_map/reshape | solution.py:73
  25.4 2.9 %copy.214 = bf16[40,16,2048]{2,0,1:T(8,128)(2,1)} copy(bf16[40,16,2048]{2,1,0:T(8,128)(2,1)S(1)} %reshape.57) | data formatting | bytes 5242880 | tf_op jit(solution)/shard_map/reshape | solution.py:73
  28.4 6.6 %collective-permute-done.1 = bf16[21,64,128]{2,0,1:T(8,128)(2,1)} collective-permute-done((bf16[21,64,128]{2,0,1:T(8,128)(2,1)S(1)}, bf16[21,64,128]{2,0,1:T(8,128)(2,1)}, u32[]{:S(2)}, u32[]{:S(2)}) %collective-permute-start.1) | collective-permute-done | bytes 344096 | tf_op jit(solution)/shard_map/ppermute | solution.py:47
  35.0 6.9 %all-to-all-start.1 = ((bf16[16,40,2048]{2,1,0:T(8,128)(2,1)}), bf16[16,40,2048]{2,1,0:T(8,128)(2,1)S(1)}, u32[]{:S(2)}, u32[]{:S(2)}) async-start(bf16[16,40,2048]{2,1,0:T(8,128)(2,1)} %bitcast.89), calls=%async_computation.1 | async-start | bytes 5242880 | tf_op jit(solution)/shard_map/all_to_all | solution.py:77
  41.9 2.9 %collective-permute-start.2 = (bf16[21,64,128]{2,0,1:T(8,128)(2,1)}, bf16[21,64,128]{2,0,1:T(8,128)(2,1)}, u32[]{:S(2)}, u32[]{:S(2)}) collective-permute-start(bf16[21,64,128]{2,0,1:T(8,128)(2,1)} %collective-permute-done.1), channel_id=1, source_target_pairs={{0,4},{4,0},{8,12},{12,8},{16,20},{20,16},{24,28},{28,24},{32,36},... | collective-permute-start | bytes 1032200 | tf_op jit(solution)/shard_map/ppermute | solution.py:47
  44.9 0.7 copy.160
  45.6 0.8 slice.78
  46.4 0.8 slice.77
  47.2 0.8 slice.99
  48.1 0.9 fusion.25
  49.0 2.1 %reduce-precision_convert_fusion = (bf16[84,32]{0,1:T(8,128)(2,1)S(1)}, bf16[84,32]{0,1:T(8,128)(2,1)S(1)}) fusion(bf16[32,64,128]{2,1,0:T(8,128)(2,1)S(1)} %all-to-all-done, bf16[21,64,128]{2,0,1:T(8,128)(2,1)} %collective-permute-done.2, bf16[21,64,128]{2,0,1:T(8,128)(2,1)} %collective-permute-done.1, bf16[21,64,128]{2,0,1:T(8,128)(2,1)} %collective-permute-done, ...), kind=kOutput, calls=%fused_computation.45 | convolution fusion | flops 49555968 | bytes 1911296 | tf_op jit(solution)/shard_map/giq,wiq->gw/dot_general | solution.py:86
  51.2 0.1 copy.161
  51.3 23.3 %all-gather.1 = bf16[4,148,128]{2,1,0:T(8,128)(2,1)S(1)} all-gather(bf16[1,148,128]{2,1,0:T(8,128)(2,1)S(1)} %copy.161), channel_id=2, replica_groups=mesh['chol'=128,'orb'=4] {'orb'}, dimensions={0}, use_global_device_ids=true | all-gather | bytes 189440 | tf_op jit(solution)/shard_map/all_gather | solution.py:91
  74.7 0.6 copy-done
  75.7 0.1 copy.165
  75.9 0.1 copy.164
  76.0 0.1 pad_maximum_fusion.3
  76.1 0.1 copy.166
  76.2 9.9 %all_gather.11 = bf16[2,4,80,64]{2,3,0,1:T(8,128)(2,1)S(1)} all-gather(bf16[2,1,80,64]{2,3,0,1:T(8,128)(2,1)S(1)} %copy.166), channel_id=1, replica_groups={{0,8,16,24},{4,12,20,28},{32,40,48,56},{36,44,52,60},{64,72,80,88},{68,..., dimensions={1}, use_global_device_ids=true | all-gather | bytes 102400 | tf_op jit(solution)/shard_map/all_gather | solution.py:105
  86.2 6.5 %collective-permute-start.6 = (bf16[640,2048]{1,0:T(8,128)(2,1)S(1)}, bf16[640,2048]{1,0:T(8,128)(2,1)}, u32[]{:S(2)}, u32[]{:S(2)}) collective-permute-start(bf16[640,2048]{1,0:T(8,128)(2,1)S(1)} %bitcast.87), channel_id=1, source_target_pairs={{0,4},{4,0},{8,12},{12,8},{16,20},{20,16},{24,28},{28,24},{32,36},... | collective-permute-start | bytes 7864328 | tf_op jit(solution)/shard_map/ppermute | solution.py:47
  92.7 0.1 copy.175
  92.8 0.1 broadcast_in_dim.23
  92.9 0.3 reshape.64
  93.3 12.3 %all_to_all.20 = bf16[8,320,64]{1,2,0:T(8,128)(2,1)} all-to-all(bf16[8,320,64]{1,2,0:T(8,128)(2,1)S(1)} %reshape.64), channel_id=1, replica_groups={{0,32,128,160,256,288,384,416},{4,36,132,164,260,292,388,420},{8,40,136..., dimensions={0} | all-to-all | bytes 655360 | tf_op jit(solution)/shard_map/all_to_all | solution.py:109
  105.6 1.3 copy.176
  107.0 0.2 pad_maximum_fusion.1
  107.2 0.6 fusion.45
  107.8 2.4 %fusion = bf16[128,2048]{1,0:T(8,128)(2,1)S(1)} fusion(f32[128,2048]{1,0:T(8,128)S(1)} %fusion.45, bf16[640,128]{1,0:T(8,128)(2,1)S(1)} %bitcast.98, bf16[640,2048]{1,0:T(8,128)(2,1)} %collective-permute-done.6), kind=kOutput, calls=%fused_computation.2 | convolution fusion | flops 336068608 | bytes 4358144 | tf_op jit(solution)/shard_map/dot_general | solution.py:115
  110.2 0.2 reshape.66
  110.4 0.5 copy.215
  110.9 0.9 reshape.67
  111.9 6.2 %all-to-all-start.3 = ((bf16[64,8,512]{2,1,0:T(8,128)(2,1)}), bf16[64,8,512]{2,1,0:T(8,128)(2,1)S(1)}, u32[]{:S(2)}, u32[]{:S(2)}) async-start(bf16[64,8,512]{2,1,0:T(8,128)(2,1)} %reshape.67), calls=%async_computation.3 | async-start | bytes 1048576 | tf_op jit(solution)/shard_map/all_to_all | solution.py:125
  118.2 4.2 %collective-permute-start.5 = (f32[20,32]{0,1:T(8,128)S(1)}, f32[20,32]{0,1:T(8,128)S(1)}, u32[]{:S(2)}, u32[]{:S(2)}) collective-permute-start(f32[20,32]{0,1:T(8,128)S(1)} %bitcast.114), channel_id=1, source_target_pairs={{0,36},{4,32},{8,44},{12,40},{16,52},{20,48},{24,60},{28,56},{32,4... | collective-permute-start | bytes 7688 | tf_op jit(solution)/shard_map/ppermute | solution.py:47
  122.5 2.1 %collective-permute-start.4 = (f32[20,32]{0,1:T(8,128)S(1)}, f32[20,32]{0,1:T(8,128)S(1)}, u32[]{:S(2)}, u32[]{:S(2)}) collective-permute-start(f32[20,32]{0,1:T(8,128)S(1)} %bitcast.112), channel_id=1, source_target_pairs={{0,32},{4,36},{8,40},{12,44},{16,48},{20,52},{24,56},{28,60},{32,0... | collective-permute-start | bytes 7688 | tf_op jit(solution)/shard_map/ppermute | solution.py:47
  124.6 2.1 %collective-permute-start.3 = (f32[20,32]{0,1:T(8,128)S(1)}, f32[20,32]{0,1:T(8,128)S(1)}, u32[]{:S(2)}, u32[]{:S(2)}) collective-permute-start(f32[20,32]{0,1:T(8,128)S(1)} %bitcast.110), channel_id=1, source_target_pairs={{0,4},{4,0},{8,12},{12,8},{16,20},{20,16},{24,28},{28,24},{32,36},... | collective-permute-start | bytes 7688 | tf_op jit(solution)/shard_map/ppermute | solution.py:47
  126.7 0.7 collective-permute-done.4
  127.5 0.2 collective-permute-done.3
  127.8 0.7 copy.181
  128.5 6.8 %all-to-all-done.3 = bf16[64,8,512]{2,1,0:T(8,128)(2,1)S(1)} async-done(((bf16[64,8,512]{2,1,0:T(8,128)(2,1)}), bf16[64,8,512]{2,1,0:T(8,128)(2,1)S(1)}, u32[]{:S(2)}, u32[]{:S(2)}) %all-to-all-start.3) | async-done | bytes 524320 | tf_op jit(solution)/shard_map/all_to_all | solution.py:125
  135.6 1.0 fusion.12
  136.6 0.7 copy.182
  (45 shorter events, 1.3 us)
Async XLA Ops:
  2.3 32.7 %all-to-all-start = ((bf16[32,64,128]{2,1,0:T(8,128)(2,1)}), bf16[32,64,128]{2,1,0:T(8,128)(2,1)S(1)}, u32[]{:S(2)}, u32[]{:S(2)}) async-start(bf16[32,64,128]{2,1,0:T(8,128)(2,1)} %broadcast_in_dim.21), calls=%async_computation | async-start | bytes 1048576 | tf_op jit(solution)/shard_map/all_to_all | solution.py:67
  14.9 13.5 %collective-permute-start = (bf16[21,64,128]{2,0,1:T(8,128)(2,1)S(1)}, bf16[21,64,128]{2,0,1:T(8,128)(2,1)}, u32[]{:S(2)}, u32[]{:S(2)}) collective-permute-start(bf16[21,64,128]{2,0,1:T(8,128)(2,1)S(1)} %pad_maximum_fusion), channel_id=1, source_target_pairs={{0,4},{4,0},{8,12},{12,8},{16,20},{20,16},{24,28},{28,24},{32,36},... | collective-permute-start | bytes 1032200 | tf_op jit(solution)/shard_map/ppermute | solution.py:47
  17.8 17.2 %collective-permute-start.1 = (bf16[21,64,128]{2,0,1:T(8,128)(2,1)S(1)}, bf16[21,64,128]{2,0,1:T(8,128)(2,1)}, u32[]{:S(2)}, u32[]{:S(2)}) collective-permute-start(bf16[21,64,128]{2,0,1:T(8,128)(2,1)S(1)} %pad_maximum_fusion), channel_id=1, source_target_pairs={{0,32},{4,36},{8,40},{12,44},{16,48},{20,52},{24,56},{28,60},{32,0... | collective-permute-start | bytes 1032200 | tf_op jit(solution)/shard_map/ppermute | solution.py:47
  35.0 9.9 %copy-start.3 = (bf16[1,64,128]{2,1,0:T(8,128)(2,1)S(1)}, bf16[1,64,128]{2,1,0:T(8,128)(2,1)}, u32[]{:S(2)}) copy-start(bf16[1,64,128]{2,1,0:T(8,128)(2,1)} %param.9) | copy-start | bytes 49156
  35.0 51.2 %all-to-all-start.1 = ((bf16[16,40,2048]{2,1,0:T(8,128)(2,1)}), bf16[16,40,2048]{2,1,0:T(8,128)(2,1)S(1)}, u32[]{:S(2)}, u32[]{:S(2)}) async-start(bf16[16,40,2048]{2,1,0:T(8,128)(2,1)} %bitcast.89), calls=%async_computation.1 | async-start | bytes 5242880 | tf_op jit(solution)/shard_map/all_to_all | solution.py:77
  41.9 5.3 %collective-permute-start.2 = (bf16[21,64,128]{2,0,1:T(8,128)(2,1)}, bf16[21,64,128]{2,0,1:T(8,128)(2,1)}, u32[]{:S(2)}, u32[]{:S(2)}) collective-permute-start(bf16[21,64,128]{2,0,1:T(8,128)(2,1)} %collective-permute-done.1), channel_id=1, source_target_pairs={{0,4},{4,0},{8,12},{12,8},{16,20},{20,16},{24,28},{28,24},{32,36},... | collective-permute-start | bytes 1032200 | tf_op jit(solution)/shard_map/ppermute | solution.py:47
  49.0 2.1 %copy-start.1 = (bf16[1,64,128]{1,2,0:T(8,128)(2,1)S(1)}, bf16[1,64,128]{1,2,0:T(8,128)(2,1)}, u32[]{:S(2)}) copy-start(bf16[1,64,128]{1,2,0:T(8,128)(2,1)} %copy.160) | copy-start | bytes 49156
  74.6 0.7 copy-start
  86.2 21.6 %collective-permute-start.6 = (bf16[640,2048]{1,0:T(8,128)(2,1)S(1)}, bf16[640,2048]{1,0:T(8,128)(2,1)}, u32[]{:S(2)}, u32[]{:S(2)}) collective-permute-start(bf16[640,2048]{1,0:T(8,128)(2,1)S(1)} %bitcast.87), channel_id=1, source_target_pairs={{0,4},{4,0},{8,12},{12,8},{16,20},{20,16},{24,28},{28,24},{32,36},... | collective-permute-start | bytes 7864328 | tf_op jit(solution)/shard_map/ppermute | solution.py:47
  110.9 24.6 %copy-start.2 = (bf16[1,64,128]{1,2,0:T(8,128)(2,1)S(1)}, bf16[1,64,128]{1,2,0:T(8,128)(2,1)}, u32[]{:S(2)}) copy-start(bf16[1,64,128]{1,2,0:T(8,128)(2,1)} %copy.160) | copy-start | bytes 49156
  111.9 23.4 %all-to-all-start.3 = ((bf16[64,8,512]{2,1,0:T(8,128)(2,1)}), bf16[64,8,512]{2,1,0:T(8,128)(2,1)S(1)}, u32[]{:S(2)}, u32[]{:S(2)}) async-start(bf16[64,8,512]{2,1,0:T(8,128)(2,1)} %reshape.67), calls=%async_computation.3 | async-start | bytes 1048576 | tf_op jit(solution)/shard_map/all_to_all | solution.py:125
  118.2 8.5 %collective-permute-start.5 = (f32[20,32]{0,1:T(8,128)S(1)}, f32[20,32]{0,1:T(8,128)S(1)}, u32[]{:S(2)}, u32[]{:S(2)}) collective-permute-start(f32[20,32]{0,1:T(8,128)S(1)} %bitcast.114), channel_id=1, source_target_pairs={{0,36},{4,32},{8,44},{12,40},{16,52},{20,48},{24,60},{28,56},{32,4... | collective-permute-start | bytes 7688 | tf_op jit(solution)/shard_map/ppermute | solution.py:47
  122.5 5.0 %collective-permute-start.4 = (f32[20,32]{0,1:T(8,128)S(1)}, f32[20,32]{0,1:T(8,128)S(1)}, u32[]{:S(2)}, u32[]{:S(2)}) collective-permute-start(f32[20,32]{0,1:T(8,128)S(1)} %bitcast.112), channel_id=1, source_target_pairs={{0,32},{4,36},{8,40},{12,44},{16,48},{20,52},{24,56},{28,60},{32,0... | collective-permute-start | bytes 7688 | tf_op jit(solution)/shard_map/ppermute | solution.py:47
  124.6 3.1 %collective-permute-start.3 = (f32[20,32]{0,1:T(8,128)S(1)}, f32[20,32]{0,1:T(8,128)S(1)}, u32[]{:S(2)}, u32[]{:S(2)}) collective-permute-start(f32[20,32]{0,1:T(8,128)S(1)} %bitcast.110), channel_id=1, source_target_pairs={{0,4},{4,0},{8,12},{12,8},{16,20},{20,16},{24,28},{28,24},{32,36},... | collective-permute-start | bytes 7688 | tf_op jit(solution)/shard_map/ppermute | solution.py:47

commit v6 on v4

--- a/solution.py
+++ b/solution.py
@@ -72,7 +72,7 @@
     chol_rows = chol_vectors.reshape(own * 2, CHIPS, rows // 2 * basis).transpose(1, 0, 2)
     chol_rows = with_layout_constraint(chol_rows, Layout((0, 1, 2)))
 
-    green, chol_rows, held = lax.optimization_barrier((green, chol_rows, held))
+    green, chol_rows, held[1] = lax.optimization_barrier((green, chol_rows, held[1]))
     chol_mine = lax.all_to_all(chol_rows, "chol", 0, 0, axis_index_groups=PLANE)
     chol_mine = chol_mine.reshape(CHIPS * own * 2, rows // 2 * basis)
 
@@ -83,13 +83,18 @@
 
     rotated = jnp.concatenate(held, axis=0)
     partial_bias = jnp.einsum("giq,wiq->gw", rotated, green, preferred_element_type=f32)
-    partial_bias = jnp.pad(partial_bias.astype(bf16), ((0, 0), (0, width - share)))
+    upper = lax.reduce_precision(partial_bias, 8, 7)
+    partial_bias = jnp.concatenate([upper, partial_bias - upper], axis=1).astype(bf16)
+    partial_bias = jnp.pad(partial_bias, ((0, 0), (0, width - 2 * share)))
     gathered = lax.all_gather(
         jnp.concatenate([walkers[0], partial_bias], axis=0), "orb", axis=0, tiled=False
     )
-    bias = jnp.sum(gathered[:, occupied:, :share].astype(f32), axis=0)
+    bias = jnp.sum(gathered[:, occupied:, : 2 * share].astype(f32), axis=0)
+    bias = bias[:, :share] + bias[:, share:]
     walker_full = gathered[:, :occupied]
-    bias, chol_mine, walker_full = lax.optimization_barrier((bias, chol_mine, walker_full))
+    bias, levels, chol_mine, walker_full = lax.optimization_barrier(
+        (bias, levels, chol_mine, walker_full)
+    )
 
     aux_field = (LEVEL_SCALE * levels - TAU_ROOT * bias).astype(bf16)
     aux_field = aux_field.reshape(2, 2, own + 1, share)[:, :, :own]
@@ -116,9 +121,9 @@
         for i, part in enumerate((chol_mine, chol_others))
     )
     potential = potential.astype(bf16).reshape(2, 2, SIDE * 2, SIDE, rows // 2 * basis)
-    potential = potential.transpose(2, 0, 3, 1, 4).reshape(HOMES, rows, basis)
+    potential = potential.transpose(2, 0, 3, 1, 4).reshape(HOMES, 2, rows // 2 * basis)
     parts = lax.all_to_all(potential, "chol", 0, 0, axis_index_groups=HOME)
-    parts = parts.reshape(SIDE, SIDE, SIDE, rows, basis)
+    parts = parts.reshape(SIDE, SIDE, SIDE, 2, rows // 2 * basis)
     total = jnp.sum(parts.astype(f32), axis=1).astype(bf16)
     total = total.reshape(CHIPS, 2, rows // 2, basis).transpose(1, 0, 2, 3)
 

time: 135 us -> 156 us (1.16)
  local copies, waits for them, and re-layouts: 19.3 us -> 39.4 us
  other arithmetic: 1.43 us -> 3.59 us
  blocking collectives: 37.7 us -> 39.8 us
  starting transfers between devices: 46.9 us -> 45.1 us
  waiting for transfers between devices: 20.8 us -> 19.1 us
    concatenate x0 -> x1, local copies, waits for them, and re-layouts: none -> 18.1 us  [shards(): rotated = jnp.concatenate(held, axis=0)]
    all_to_all x1, waiting for transfers between devices: 6.59 us -> 0.01 us  [shards(): chol_mine = lax.all_to_all(chol_rows, 'chol', 0, 0, axis_index_groups=PLANE)]
    all_to_all x1, waiting for transfers between devices: 0.01 us -> 3.6 us  [shards(): green = lax.all_to_all(green, 'chol', 0, 0, axis_index_groups=GREEN)]
    ppermute x7, starting transfers between devices: 21.5 us -> 24.7 us  [to_mate(): lax.ppermute(array, 'chol', [(i, i ^ step) for i in range(len(PLACES))])]
    all_to_all x1, blocking collectives: 14.4 us -> 17.4 us  [shards(): aux_all = lax.all_to_all(aux_sent, 'chol', 0, 0, axis_index_groups=BLOCK)]
    all_to_all x1, starting transfers between devices: 6.94 us -> 4.03 us  [shards(): chol_mine = lax.all_to_all(chol_rows, 'chol', 0, 0, axis_index_groups=PLANE)]
    all_to_all x1, starting transfers between devices: 7.84 us -> 5.76 us  [shards(): parts = lax.all_to_all(potential, 'chol', 0, 0, axis_index_groups=HOME)]
    unnamed x18 -> x24, local copies, waits for them, and re-layouts: 4.02 us -> 5.49 us
  transfers between devices with their start and end apart: 10 -> 10, of which waited for: 4 -> 5; matrix products, arithmetic and copies ran while one was open for 14% -> 27% of each run, Pallas kernels for 0% -> 0%
where the time goes in v6:
time: 156 us; the launch traced here: 154 us
  starting transfers between devices  45.1 us (29%)
  blocking collectives  39.8 us (26%)
  local copies, waits for them, and re-layouts  39.4 us (25%)
  waiting for transfers between devices  19.1 us (12%)
  matrix products  6.08 us (4%)
  other arithmetic  3.59 us (2%)
    ppermute x7, starting transfers between devices, to_mate(): lax.ppermute(array, 'chol', [(i, i ^ step) for i in range(len(PLACES))])  24.7 us
    all_gather x1, blocking collectives, shards(): lax.all_gather(jnp.concatenate([walkers[0], partial_bias], axis=0), 'orb'...  22.4 us
    concatenate x1, local copies, waits for them, and re-layouts, shards(): rotated = jnp.concatenate(held, axis=0)  18.1 us
    all_to_all x1, blocking collectives, shards(): aux_all = lax.all_to_all(aux_sent, 'chol', 0, 0, axis_index_groups=BLOCK)  17.4 us
    all_to_all x1, starting transfers between devices, shards(): green = lax.all_to_all(green, 'chol', 0, 0, axis_index_groups=GREEN)  10.6 us
    ppermute x7, waiting for transfers between devices, to_mate(): lax.ppermute(array, 'chol', [(i, i ^ step) for i in range(len(PLACES))])  8.75 us
    reshape x2, local copies, waits for them, and re-layouts, shards(): chol_vectors.reshape(own * 2, CHIPS, rows // 2 * basis).transpose(1, 0, 2)  7.05 us
    all_to_all x1, waiting for transfers between devices, shards(): parts = lax.all_to_all(potential, 'chol', 0, 0, axis_index_groups=HOME)  6.79 us
  transfers between devices with their start and end apart: 10, of which 5 were waited for; matrix products, arithmetic and copies ran while one was open for 27% of the time, Pallas kernels for 0%

profile of v6, /device:TPU:1, one launch (start us, length us, event | category | flops | bytes accessed | tf_op | source)
XLA Modules:
  0.0 154.3 jit_solution(13084950200882509907)
XLA Ops:
  0.6 1.6 %broadcast_in_dim.23 = bf16[32,64,128]{2,1,0:T(8,128)(2,1)} broadcast(bf16[64,128]{1,0:T(8,128)(2,1)} %bitcast.115), dimensions={1,2} | broadcast | bytes 540672 | tf_op jit(solution)/shard_map/broadcast_in_dim | solution.py:65
  2.3 10.6 %all-to-all-start = ((bf16[32,64,128]{2,1,0:T(8,128)(2,1)}), bf16[32,64,128]{2,1,0:T(8,128)(2,1)S(1)}, u32[]{:S(2)}, u32[]{:S(2)}) async-start(bf16[32,64,128]{2,1,0:T(8,128)(2,1)} %broadcast_in_dim.23), calls=%async_computation | async-start | bytes 1048576 | tf_op jit(solution)/shard_map/all_to_all | solution.py:66
  12.8 1.2 copy.162
  14.0 0.7 convert_bitcast_fusion
  14.8 0.8 pad_maximum_fusion
  15.7 2.9 %collective-permute-start = (bf16[21,64,128]{2,0,1:T(8,128)(2,1)}, bf16[21,64,128]{2,0,1:T(8,128)(2,1)}, u32[]{:S(2)}, u32[]{:S(2)}) collective-permute-start(bf16[21,64,128]{2,0,1:T(8,128)(2,1)} %pad_maximum_fusion), channel_id=1, source_target_pairs={{0,4},{4,0},{8,12},{12,8},{16,20},{20,16},{24,28},{28,24},{32,36},... | collective-permute-start | bytes 1032200 | tf_op jit(solution)/shard_map/ppermute | solution.py:46
  18.5 4.1 %reshape.57 = bf16[40,16,2048]{2,1,0:T(8,128)(2,1)S(1)} reshape(bf16[20,128,512]{2,1,0:T(8,128)(2,1)} %param.8) | data formatting | bytes 5242880 | tf_op jit(solution)/shard_map/reshape | solution.py:72
  22.6 2.9 %copy.220 = bf16[40,16,2048]{2,0,1:T(8,128)(2,1)} copy(bf16[40,16,2048]{2,1,0:T(8,128)(2,1)S(1)} %reshape.57) | data formatting | bytes 5242880 | tf_op jit(solution)/shard_map/reshape | solution.py:72
  25.6 3.6 %all-to-all-done = bf16[32,64,128]{2,1,0:T(8,128)(2,1)S(1)} async-done(((bf16[32,64,128]{2,1,0:T(8,128)(2,1)}), bf16[32,64,128]{2,1,0:T(8,128)(2,1)S(1)}, u32[]{:S(2)}, u32[]{:S(2)}) %all-to-all-start) | async-done | bytes 524320 | tf_op jit(solution)/shard_map/all_to_all | solution.py:66
  29.2 4.0 %all-to-all-start.1 = ((bf16[16,40,2048]{2,1,0:T(8,128)(2,1)}), bf16[16,40,2048]{2,1,0:T(8,128)(2,1)S(1)}, u32[]{:S(2)}, u32[]{:S(2)}) async-start(bf16[16,40,2048]{2,1,0:T(8,128)(2,1)} %bitcast.95), calls=%async_computation.1 | async-start | bytes 5242880 | tf_op jit(solution)/shard_map/all_to_all | solution.py:76
  33.2 2.7 %collective-permute-start.1 = (bf16[21,64,128]{2,0,1:T(8,128)(2,1)}, bf16[21,64,128]{2,0,1:T(8,128)(2,1)}, u32[]{:S(2)}, u32[]{:S(2)}) collective-permute-start(bf16[21,64,128]{2,0,1:T(8,128)(2,1)} %pad_maximum_fusion), channel_id=1, source_target_pairs={{0,32},{4,36},{8,40},{12,44},{16,48},{20,52},{24,56},{28,60},{32,0... | collective-permute-start | bytes 1032200 | tf_op jit(solution)/shard_map/ppermute | solution.py:46
  36.0 7.8 %collective-permute-done.1 = bf16[21,64,128]{2,0,1:T(8,128)(2,1)} collective-permute-done((bf16[21,64,128]{2,0,1:T(8,128)(2,1)}, bf16[21,64,128]{2,0,1:T(8,128)(2,1)}, u32[]{:S(2)}, u32[]{:S(2)}) %collective-permute-start.1) | collective-permute-done | bytes 344096 | tf_op jit(solution)/shard_map/ppermute | solution.py:46
  43.8 5.1 %collective-permute-start.2 = (bf16[21,64,128]{2,0,1:T(8,128)(2,1)}, bf16[21,64,128]{2,0,1:T(8,128)(2,1)}, u32[]{:S(2)}, u32[]{:S(2)}) collective-permute-start(bf16[21,64,128]{2,0,1:T(8,128)(2,1)} %collective-permute-done.1), channel_id=1, source_target_pairs={{0,4},{4,0},{8,12},{12,8},{16,20},{20,16},{24,28},{28,24},{32,36},... | collective-permute-start | bytes 1032200 | tf_op jit(solution)/shard_map/ppermute | solution.py:46
  48.9 1.4 copy.158
  50.3 0.6 slice_bitcast_fusion
  50.9 0.8 slice.103
  51.7 0.6 copy.223
  52.3 0.8 slice.104
  53.1 0.6 copy.222
  53.7 0.8 slice.80
  54.5 18.1 %concatenate.34 = bf16[84,64,128]{2,0,1:T(8,128)(2,1)} concatenate(bf16[20,64,128]{2,0,1:T(8,128)(2,1)S(1)} %copy.162, bf16[1,64,128]{2,0,1:T(2,128)(2,1)} %copy-done.1, bf16[21,64,128]{2,0,1:T(8,128)(2,1)} %collective-permute-done, bf16[21,64,128]{2,0,1:T(8,128)(2,1)} %collective-permute-done.1, bf16[21,64,128]{2,0,1:T(8,128)(2,1)} %collective-permute-done.2), dimensions={0} | concatenate | bytes 2752512 | tf_op jit(solution)/shard_map/concatenate | solution.py:84
  72.7 2.0 %reduce-precision_convert_fusion = (bf16[84,32]{0,1:T(8,128)(2,1)S(1)}, bf16[84,32]{0,1:T(8,128)(2,1)S(1)}) fusion(bf16[84,64,128]{2,0,1:T(8,128)(2,1)} %concatenate.34, bf16[32,64,128]{2,1,0:T(8,128)(2,1)S(1)} %all-to-all-done), kind=kOutput, calls=%fused_computation.36 | convolution fusion | flops 44050944 | bytes 1911296 | tf_op jit(solution)/shard_map/giq,wiq->gw/dot_general | solution.py:85
  74.7 0.8 maximum_bitcast_fusion
  75.7 22.4 %all-gather.1 = bf16[4,148,128]{2,1,0:T(8,128)(2,1)S(1)} all-gather(bf16[1,148,128]{2,1,0:T(8,128)(2,1)S(1)} %copy.165), channel_id=2, replica_groups=mesh['chol'=128,'orb'=4] {'orb'}, dimensions={0}, use_global_device_ids=true | all-gather | bytes 189440 | tf_op jit(solution)/shard_map/all_gather | solution.py:89
  98.4 0.9 fusion.13
  99.5 5.6 %collective-permute-start.6 = (bf16[640,2048]{1,0:T(8,128)(2,1)S(1)}, bf16[640,2048]{1,0:T(8,128)(2,1)}, u32[]{:S(2)}, u32[]{:S(2)}) collective-permute-start(bf16[640,2048]{1,0:T(8,128)(2,1)S(1)} %bitcast.93), channel_id=1, source_target_pairs={{0,4},{4,0},{8,12},{12,8},{16,20},{20,16},{24,28},{28,24},{32,36},... | collective-permute-start | bytes 7864328 | tf_op jit(solution)/shard_map/ppermute | solution.py:46
  105.3 0.1 copy.177
  105.4 0.1 copy.176
  105.6 0.1 pad_maximum_fusion.3
  105.8 0.1 broadcast_in_dim.25
  105.9 17.4 %all_to_all.20 = bf16[32,80,64]{1,2,0:T(8,128)(2,1)} all-to-all(bf16[32,80,64]{1,2,0:T(8,128)(2,1)S(1)} %bitcast.98), channel_id=1, replica_groups={{0,8,16,24,32,40,48,56,128,136,144,152,160,168,176,184,256,264,272,280,..., dimensions={0} | all-to-all | bytes 655360 | tf_op jit(solution)/shard_map/all_to_all | solution.py:109
  123.3 1.3 copy.179
  124.7 0.2 pad_maximum_fusion.1
  124.9 0.6 fusion.32
  125.5 2.3 %fusion = bf16[128,2048]{1,0:T(8,128)(2,1)S(1)} fusion(f32[128,2048]{1,0:T(8,128)S(1)} %fusion.32, bf16[640,128]{1,0:T(8,128)(2,1)S(1)} %bitcast.104, bf16[640,2048]{1,0:T(8,128)(2,1)} %collective-permute-done.6), kind=kOutput, calls=%fused_computation.2 | convolution fusion | flops 336068608 | bytes 4358144 | tf_op jit(solution)/shard_map/dot_general | solution.py:115
  127.9 0.2 reshape.66
  128.1 1.4 copy.182
  129.5 5.8 %all-to-all-start.3 = ((bf16[64,2,2048]{2,1,0:T(2,128)(2,1)}), bf16[64,2,2048]{2,1,0:T(2,128)(2,1)S(1)}, u32[]{:S(2)}, u32[]{:S(2)}) async-start(bf16[64,2,2048]{2,1,0:T(2,128)(2,1)} %bitcast.34), calls=%async_computation.3 | async-start | bytes 1048576 | tf_op jit(solution)/shard_map/all_to_all | solution.py:125
  135.4 4.2 %collective-permute-start.5 = (f32[20,32]{0,1:T(8,128)S(1)}, f32[20,32]{0,1:T(8,128)S(1)}, u32[]{:S(2)}, u32[]{:S(2)}) collective-permute-start(f32[20,32]{0,1:T(8,128)S(1)} %bitcast.120), channel_id=1, source_target_pairs={{0,36},{4,32},{8,44},{12,40},{16,52},{20,48},{24,60},{28,56},{32,4... | collective-permute-start | bytes 7688 | tf_op jit(solution)/shard_map/ppermute | solution.py:46
  139.6 2.1 %collective-permute-start.4 = (f32[20,32]{0,1:T(8,128)S(1)}, f32[20,32]{0,1:T(8,128)S(1)}, u32[]{:S(2)}, u32[]{:S(2)}) collective-permute-start(f32[20,32]{0,1:T(8,128)S(1)} %bitcast.118), channel_id=1, source_target_pairs={{0,32},{4,36},{8,40},{12,44},{16,48},{20,52},{24,56},{28,60},{32,0... | collective-permute-start | bytes 7688 | tf_op jit(solution)/shard_map/ppermute | solution.py:46
  141.7 2.1 %collective-permute-start.3 = (f32[20,32]{0,1:T(8,128)S(1)}, f32[20,32]{0,1:T(8,128)S(1)}, u32[]{:S(2)}, u32[]{:S(2)}) collective-permute-start(f32[20,32]{0,1:T(8,128)S(1)} %bitcast.116), channel_id=1, source_target_pairs={{0,4},{4,0},{8,12},{12,8},{16,20},{20,16},{24,28},{28,24},{32,36},... | collective-permute-start | bytes 7688 | tf_op jit(solution)/shard_map/ppermute | solution.py:46
  143.9 0.7 collective-permute-done.4
  144.6 0.2 collective-permute-done.3
  145.0 0.7 copy.186
  145.7 6.8 %all-to-all-done.3 = bf16[64,2,2048]{2,1,0:T(2,128)(2,1)S(1)} async-done(((bf16[64,2,2048]{2,1,0:T(2,128)(2,1)}), bf16[64,2,2048]{2,1,0:T(2,128)(2,1)S(1)}, u32[]{:S(2)}, u32[]{:S(2)}) %all-to-all-start.3) | async-done | bytes 524320 | tf_op jit(solution)/shard_map/all_to_all | solution.py:125
  152.5 0.7 reduce_sum.22
  153.4 0.2 fusion.4
  153.6 0.7 copy.187
  (49 shorter events, 1.3 us)
Async XLA Ops:
  2.3 26.9 %all-to-all-start = ((bf16[32,64,128]{2,1,0:T(8,128)(2,1)}), bf16[32,64,128]{2,1,0:T(8,128)(2,1)S(1)}, u32[]{:S(2)}, u32[]{:S(2)}) async-start(bf16[32,64,128]{2,1,0:T(8,128)(2,1)} %broadcast_in_dim.23), calls=%async_computation | async-start | bytes 1048576 | tf_op jit(solution)/shard_map/all_to_all | solution.py:66
  14.8 0.9 copy-start.1
  15.7 9.9 %collective-permute-start = (bf16[21,64,128]{2,0,1:T(8,128)(2,1)}, bf16[21,64,128]{2,0,1:T(8,128)(2,1)}, u32[]{:S(2)}, u32[]{:S(2)}) collective-permute-start(bf16[21,64,128]{2,0,1:T(8,128)(2,1)} %pad_maximum_fusion), channel_id=1, source_target_pairs={{0,4},{4,0},{8,12},{12,8},{16,20},{20,16},{24,28},{28,24},{32,36},... | collective-permute-start | bytes 1032200 | tf_op jit(solution)/shard_map/ppermute | solution.py:46
  29.2 70.2 %all-to-all-start.1 = ((bf16[16,40,2048]{2,1,0:T(8,128)(2,1)}), bf16[16,40,2048]{2,1,0:T(8,128)(2,1)S(1)}, u32[]{:S(2)}, u32[]{:S(2)}) async-start(bf16[16,40,2048]{2,1,0:T(8,128)(2,1)} %bitcast.95), calls=%async_computation.1 | async-start | bytes 5242880 | tf_op jit(solution)/shard_map/all_to_all | solution.py:76
  33.2 10.6 %collective-permute-start.1 = (bf16[21,64,128]{2,0,1:T(8,128)(2,1)}, bf16[21,64,128]{2,0,1:T(8,128)(2,1)}, u32[]{:S(2)}, u32[]{:S(2)}) collective-permute-start(bf16[21,64,128]{2,0,1:T(8,128)(2,1)} %pad_maximum_fusion), channel_id=1, source_target_pairs={{0,32},{4,36},{8,40},{12,44},{16,48},{20,52},{24,56},{28,60},{32,0... | collective-permute-start | bytes 1032200 | tf_op jit(solution)/shard_map/ppermute | solution.py:46
  43.8 8.6 %collective-permute-start.2 = (bf16[21,64,128]{2,0,1:T(8,128)(2,1)}, bf16[21,64,128]{2,0,1:T(8,128)(2,1)}, u32[]{:S(2)}, u32[]{:S(2)}) collective-permute-start(bf16[21,64,128]{2,0,1:T(8,128)(2,1)} %collective-permute-done.1), channel_id=1, source_target_pairs={{0,4},{4,0},{8,12},{12,8},{16,20},{20,16},{24,28},{28,24},{32,36},... | collective-permute-start | bytes 1032200 | tf_op jit(solution)/shard_map/ppermute | solution.py:46
  72.7 25.7 %copy-start.3 = (bf16[21,128]{1,0:T(8,128)(2,1)S(1)}, bf16[21,128]{1,0:T(8,128)(2,1)}, u32[]{:S(2)}) copy-start(bf16[21,128]{1,0:T(8,128)(2,1)} %slice_bitcast_fusion) | copy-start | bytes 16132
  72.7 25.7 %copy-start.4 = (bf16[1,21,128]{2,1,0:T(8,128)(2,1)S(1)}, bf16[1,21,128]{2,1,0:T(8,128)(2,1)}, u32[]{:S(2)}) copy-start(bf16[1,21,128]{2,1,0:T(8,128)(2,1)} %copy.223) | copy-start | bytes 16132
  72.7 25.7 %copy-start.5 = (bf16[1,21,128]{2,1,0:T(8,128)(2,1)S(1)}, bf16[1,21,128]{2,1,0:T(8,128)(2,1)}, u32[]{:S(2)}) copy-start(bf16[1,21,128]{2,1,0:T(8,128)(2,1)} %copy.222) | copy-start | bytes 16132
  98.1 26.6 %copy-start = (bf16[4,148,128]{2,1,0:T(8,128)(2,1)}, bf16[4,148,128]{2,1,0:T(8,128)(2,1)S(1)}, u32[]{:S(2)}) copy-start(bf16[4,148,128]{2,1,0:T(8,128)(2,1)S(1)} %all-gather.1) | copy-start | bytes 454660
  99.5 26.1 %collective-permute-start.6 = (bf16[640,2048]{1,0:T(8,128)(2,1)S(1)}, bf16[640,2048]{1,0:T(8,128)(2,1)}, u32[]{:S(2)}, u32[]{:S(2)}) collective-permute-start(bf16[640,2048]{1,0:T(8,128)(2,1)S(1)} %bitcast.93), channel_id=1, source_target_pairs={{0,4},{4,0},{8,12},{12,8},{16,20},{20,16},{24,28},{28,24},{32,36},... | collective-permute-start | bytes 7864328 | tf_op jit(solution)/shard_map/ppermute | solution.py:46
  128.1 25.3 %slice-start = ((bf16[4,148,128]{2,1,0:T(8,128)(2,1)}), bf16[4,64,128]{2,1,0:T(8,128)(2,1)S(1)}, s32[]{:S(2)}) async-start(bf16[4,148,128]{2,1,0:T(8,128)(2,1)} %copy-done), calls=%async_computation.4 | async-start | bytes 131072 | tf_op jit(solution)/shard_map/slice | solution.py:94
  128.1 25.3 %copy-start.2 = (bf16[1,64,128]{1,2,0:T(8,128)(2,1)S(1)}, bf16[1,64,128]{1,2,0:T(8,128)(2,1)}, u32[]{:S(2)}) copy-start(bf16[1,64,128]{1,2,0:T(8,128)(2,1)} %copy.158) | copy-start | bytes 49156
  129.5 23.0 %all-to-all-start.3 = ((bf16[64,2,2048]{2,1,0:T(2,128)(2,1)}), bf16[64,2,2048]{2,1,0:T(2,128)(2,1)S(1)}, u32[]{:S(2)}, u32[]{:S(2)}) async-start(bf16[64,2,2048]{2,1,0:T(2,128)(2,1)} %bitcast.34), calls=%async_computation.3 | async-start | bytes 1048576 | tf_op jit(solution)/shard_map/all_to_all | solution.py:125
  135.4 8.5 %collective-permute-start.5 = (f32[20,32]{0,1:T(8,128)S(1)}, f32[20,32]{0,1:T(8,128)S(1)}, u32[]{:S(2)}, u32[]{:S(2)}) collective-permute-start(f32[20,32]{0,1:T(8,128)S(1)} %bitcast.120), channel_id=1, source_target_pairs={{0,36},{4,32},{8,44},{12,40},{16,52},{20,48},{24,60},{28,56},{32,4... | collective-permute-start | bytes 7688 | tf_op jit(solution)/shard_map/ppermute | solution.py:46
  139.6 5.0 %collective-permute-start.4 = (f32[20,32]{0,1:T(8,128)S(1)}, f32[20,32]{0,1:T(8,128)S(1)}, u32[]{:S(2)}, u32[]{:S(2)}) collective-permute-start(f32[20,32]{0,1:T(8,128)S(1)} %bitcast.118), channel_id=1, source_target_pairs={{0,32},{4,36},{8,40},{12,44},{16,48},{20,52},{24,56},{28,60},{32,0... | collective-permute-start | bytes 7688 | tf_op jit(solution)/shard_map/ppermute | solution.py:46
  141.7 3.1 %collective-permute-start.3 = (f32[20,32]{0,1:T(8,128)S(1)}, f32[20,32]{0,1:T(8,128)S(1)}, u32[]{:S(2)}, u32[]{:S(2)}) collective-permute-start(f32[20,32]{0,1:T(8,128)S(1)} %bitcast.116), channel_id=1, source_target_pairs={{0,4},{4,0},{8,12},{12,8},{16,20},{20,16},{24,28},{28,24},{32,36},... | collective-permute-start | bytes 7688 | tf_op jit(solution)/shard_map/ppermute | solution.py:46

commit v7 on v6

--- a/solution.py
+++ b/solution.py
@@ -67,15 +67,18 @@
 
     levels = jnp.pad(field_levels.astype(bf16).T, ((0, occupied - own), (0, 0)))
     sent = jnp.concatenate([rotated_chol, levels[None]], axis=0)
-    held = [sent, to_mate(sent, 1), to_mate(sent, 2)]
+    held = [sent, to_mate(sent, 1)]
 
     chol_rows = chol_vectors.reshape(own * 2, CHIPS, rows // 2 * basis).transpose(1, 0, 2)
     chol_rows = with_layout_constraint(chol_rows, Layout((0, 1, 2)))
 
-    green, chol_rows, held[1] = lax.optimization_barrier((green, chol_rows, held[1]))
+    green, chol_rows, held[0], held[1] = lax.optimization_barrier(
+        (green, chol_rows, held[0], held[1])
+    )
     chol_mine = lax.all_to_all(chol_rows, "chol", 0, 0, axis_index_groups=PLANE)
     chol_mine = chol_mine.reshape(CHIPS * own * 2, rows // 2 * basis)
 
+    held.append(to_mate(held[0], 2))
     held.append(to_mate(held[2], 1))
     levels = jnp.concatenate([h[own, : own + 1] for h in held], axis=0)
     chosen = lax.dynamic_index_in_dim(jnp.asarray(SHARES, bf16), zl * 2 + core, 0, keepdims=False)

time: 156 us -> 134 us (0.86)
  local copies, waits for them, and re-layouts: 39.4 us -> 19.4 us
  starting transfers between devices: 45.1 us -> 42.9 us
    concatenate x1 -> x0, local copies, waits for them, and re-layouts: 18.1 us -> none  [shards(): rotated = jnp.concatenate(held, axis=0)]
    ppermute x7, starting transfers between devices: 24.7 us -> 22.4 us  [to_mate(): lax.ppermute(array, 'chol', [(i, i ^ step) for i in range(len(PLACES))])]
    unnamed x24 -> x20, local copies, waits for them, and re-layouts: 5.49 us -> 4.17 us
  transfers between devices with their start and end apart: 10 -> 10, of which waited for: 5 -> 5; matrix products, arithmetic and copies ran while one was open for 27% -> 15% of each run, Pallas kernels for 0% -> 0%
where the time goes in v7:
time: 134 us; the launch traced here: 133 us
  starting transfers between devices  42.9 us (32%)
  blocking collectives  41.3 us (31%)
  waiting for transfers between devices  20.4 us (15%)
  local copies, waits for them, and re-layouts  19.4 us (14%)
  matrix products  6.14 us (5%)
  other arithmetic  2.07 us (2%)
    all_gather x1, blocking collectives, shards(): lax.all_gather(jnp.concatenate([walkers[0], partial_bias], axis=0), 'orb'...  23.6 us
    ppermute x7, starting transfers between devices, to_mate(): lax.ppermute(array, 'chol', [(i, i ^ step) for i in range(len(PLACES))])  22.4 us
    all_to_all x1, blocking collectives, shards(): aux_all = lax.all_to_all(aux_sent, 'chol', 0, 0, axis_index_groups=BLOCK)  17.7 us
    all_to_all x1, starting transfers between devices, shards(): green = lax.all_to_all(green, 'chol', 0, 0, axis_index_groups=GREEN)  10.6 us
    ppermute x7, waiting for transfers between devices, to_mate(): lax.ppermute(array, 'chol', [(i, i ^ step) for i in range(len(PLACES))])  9.27 us
    reshape x2, local copies, waits for them, and re-layouts, shards(): chol_vectors.reshape(own * 2, CHIPS, rows // 2 * basis).transpose(1, 0, 2)  7.04 us
    all_to_all x1, waiting for transfers between devices, shards(): parts = lax.all_to_all(potential, 'chol', 0, 0, axis_index_groups=HOME)  6.8 us
    all_to_all x1, starting transfers between devices, shards(): parts = lax.all_to_all(potential, 'chol', 0, 0, axis_index_groups=HOME)  5.77 us
  transfers between devices with their start and end apart: 10, of which 5 were waited for; matrix products, arithmetic and copies ran while one was open for 15% of the time, Pallas kernels for 0%

profile of v7, /device:TPU:1, one launch (start us, length us, event | category | flops | bytes accessed | tf_op | source)
XLA Modules:
  0.0 133.3 jit_solution(1080400013763189272)
XLA Ops:
  0.6 1.6 %broadcast_in_dim.22 = bf16[32,64,128]{2,1,0:T(8,128)(2,1)} broadcast(bf16[64,128]{1,0:T(8,128)(2,1)} %bitcast.113), dimensions={1,2} | broadcast | bytes 540672 | tf_op jit(solution)/shard_map/broadcast_in_dim | solution.py:65
  2.3 10.6 %all-to-all-start = ((bf16[32,64,128]{2,1,0:T(8,128)(2,1)}), bf16[32,64,128]{2,1,0:T(8,128)(2,1)S(1)}, u32[]{:S(2)}, u32[]{:S(2)}) async-start(bf16[32,64,128]{2,1,0:T(8,128)(2,1)} %broadcast_in_dim.22), calls=%async_computation | async-start | bytes 1048576 | tf_op jit(solution)/shard_map/all_to_all | solution.py:66
  12.8 0.7 convert_bitcast_fusion
  13.6 1.2 copy.151
  14.8 0.1 pad_maximum_fusion
  14.9 2.9 %collective-permute-start = (bf16[21,64,128]{2,0,1:T(8,128)(2,1)S(1)}, bf16[21,64,128]{2,0,1:T(8,128)(2,1)}, u32[]{:S(2)}, u32[]{:S(2)}) collective-permute-start(bf16[21,64,128]{2,0,1:T(8,128)(2,1)S(1)} %pad_maximum_fusion), channel_id=1, source_target_pairs={{0,4},{4,0},{8,12},{12,8},{16,20},{20,16},{24,28},{28,24},{32,36},... | collective-permute-start | bytes 1032200 | tf_op jit(solution)/shard_map/ppermute | solution.py:46
  17.8 4.1 %reshape.57 = bf16[40,16,2048]{2,1,0:T(8,128)(2,1)S(1)} reshape(bf16[20,128,512]{2,1,0:T(8,128)(2,1)} %param.8) | data formatting | bytes 5242880 | tf_op jit(solution)/shard_map/reshape | solution.py:72
  21.9 2.9 %copy.211 = bf16[40,16,2048]{2,0,1:T(8,128)(2,1)} copy(bf16[40,16,2048]{2,1,0:T(8,128)(2,1)S(1)} %reshape.57) | data formatting | bytes 5242880 | tf_op jit(solution)/shard_map/reshape | solution.py:72
  24.8 4.3 %all-to-all-done = bf16[32,64,128]{2,1,0:T(8,128)(2,1)S(1)} async-done(((bf16[32,64,128]{2,1,0:T(8,128)(2,1)}), bf16[32,64,128]{2,1,0:T(8,128)(2,1)S(1)}, u32[]{:S(2)}, u32[]{:S(2)}) %all-to-all-start) | async-done | bytes 524320 | tf_op jit(solution)/shard_map/all_to_all | solution.py:66
  29.2 4.2 %all-to-all-start.1 = ((bf16[16,40,2048]{2,1,0:T(8,128)(2,1)}), bf16[16,40,2048]{2,1,0:T(8,128)(2,1)S(1)}, u32[]{:S(2)}, u32[]{:S(2)}) async-start(bf16[16,40,2048]{2,1,0:T(8,128)(2,1)} %bitcast.93), calls=%async_computation.1 | async-start | bytes 5242880 | tf_op jit(solution)/shard_map/all_to_all | solution.py:78
  33.3 2.0 %collective-permute-start.1 = (bf16[21,64,128]{2,0,1:T(8,128)(2,1)S(1)}, bf16[21,64,128]{2,0,1:T(8,128)(2,1)}, u32[]{:S(2)}, u32[]{:S(2)}) collective-permute-start(bf16[21,64,128]{2,0,1:T(8,128)(2,1)S(1)} %pad_maximum_fusion), channel_id=1, source_target_pairs={{0,32},{4,36},{8,40},{12,44},{16,48},{20,52},{24,56},{28,60},{32,0... | collective-permute-start | bytes 1032200 | tf_op jit(solution)/shard_map/ppermute | solution.py:46
  35.4 8.3 %collective-permute-done.1 = bf16[21,64,128]{2,0,1:T(8,128)(2,1)} collective-permute-done((bf16[21,64,128]{2,0,1:T(8,128)(2,1)S(1)}, bf16[21,64,128]{2,0,1:T(8,128)(2,1)}, u32[]{:S(2)}, u32[]{:S(2)}) %collective-permute-start.1) | collective-permute-done | bytes 344096 | tf_op jit(solution)/shard_map/ppermute | solution.py:46
  43.7 5.1 %collective-permute-start.2 = (bf16[21,64,128]{2,0,1:T(8,128)(2,1)}, bf16[21,64,128]{2,0,1:T(8,128)(2,1)}, u32[]{:S(2)}, u32[]{:S(2)}) collective-permute-start(bf16[21,64,128]{2,0,1:T(8,128)(2,1)} %collective-permute-done.1), channel_id=1, source_target_pairs={{0,4},{4,0},{8,12},{12,8},{16,20},{20,16},{24,28},{28,24},{32,36},... | collective-permute-start | bytes 1032200 | tf_op jit(solution)/shard_map/ppermute | solution.py:46
  48.8 0.7 copy.149
  49.6 0.8 slice.80
  50.4 0.6 copy_bitcast_fusion.4
  51.0 0.8 slice.102
  51.8 2.1 %reduce-precision_convert_fusion = (bf16[84,32]{0,1:T(8,128)(2,1)S(1)}, bf16[84,32]{0,1:T(8,128)(2,1)S(1)}) fusion(bf16[32,64,128]{2,1,0:T(8,128)(2,1)S(1)} %all-to-all-done, bf16[21,64,128]{2,0,1:T(8,128)(2,1)} %collective-permute-done.2, bf16[21,64,128]{2,0,1:T(8,128)(2,1)} %collective-permute-done.1, bf16[21,64,128]{2,0,1:T(8,128)(2,1)} %collective-permute-done, ...), kind=kOutput, calls=%fused_computation.44 | convolution fusion | flops 49555968 | bytes 1911296 | tf_op jit(solution)/shard_map/giq,wiq->gw/dot_general | solution.py:88
  53.9 0.1 maximum_bitcast_fusion
  54.0 0.1 copy.154
  54.1 23.6 %all-gather.1 = bf16[4,148,128]{2,1,0:T(8,128)(2,1)S(1)} all-gather(bf16[1,148,128]{2,1,0:T(8,128)(2,1)S(1)} %copy.154), channel_id=2, replica_groups=mesh['chol'=128,'orb'=4] {'orb'}, dimensions={0}, use_global_device_ids=true | all-gather | bytes 189440 | tf_op jit(solution)/shard_map/all_gather | solution.py:92
  77.9 0.8 slice.103
  78.7 1.0 fusion.24
  79.8 4.0 %collective-permute-start.6 = (bf16[640,2048]{1,0:T(8,128)(2,1)S(1)}, bf16[640,2048]{1,0:T(8,128)(2,1)}, u32[]{:S(2)}, u32[]{:S(2)}) collective-permute-start(bf16[640,2048]{1,0:T(8,128)(2,1)S(1)} %bitcast.91), channel_id=1, source_target_pairs={{0,4},{4,0},{8,12},{12,8},{16,20},{20,16},{24,28},{28,24},{32,36},... | collective-permute-start | bytes 7864328 | tf_op jit(solution)/shard_map/ppermute | solution.py:46
  84.0 0.1 copy.166
  84.1 0.1 copy.165
  84.3 0.1 pad_maximum_fusion.3
  84.4 0.1 copy.167
  84.5 0.1 broadcast_in_dim.25
  84.6 17.7 %all_to_all.20 = bf16[32,80,64]{1,2,0:T(8,128)(2,1)} all-to-all(bf16[32,80,64]{1,2,0:T(8,128)(2,1)S(1)} %bitcast.96), channel_id=1, replica_groups={{0,8,16,24,32,40,48,56,128,136,144,152,160,168,176,184,256,264,272,280,..., dimensions={0} | all-to-all | bytes 655360 | tf_op jit(solution)/shard_map/all_to_all | solution.py:112
  102.3 1.3 %copy.168 = bf16[32,80,64]{2,1,0:T(8,128)(2,1)S(1)} copy(bf16[32,80,64]{1,2,0:T(8,128)(2,1)} %all_to_all.20) | data formatting | bytes 655360 | tf_op jit(solution)/shard_map/all_to_all | solution.py:112
  103.7 0.2 pad_maximum_fusion.1
  103.9 0.6 fusion.44
  104.6 2.3 %fusion = bf16[128,2048]{1,0:T(8,128)(2,1)S(1)} fusion(f32[128,2048]{1,0:T(8,128)S(1)} %fusion.44, bf16[640,128]{1,0:T(8,128)(2,1)S(1)} %bitcast.102, bf16[640,2048]{1,0:T(8,128)(2,1)} %collective-permute-done.6), kind=kOutput, calls=%fused_computation.2 | convolution fusion | flops 336068608 | bytes 4358144 | tf_op jit(solution)/shard_map/dot_general | solution.py:118
  106.9 0.2 reshape.66
  107.1 1.3 %copy.171 = bf16[2,2,8,4,2048]{4,1,3,0,2:T(2,128)(2,1)} copy(bf16[2,2,8,4,2048]{4,3,2,1,0:T(4,128)(2,1)S(1)} %reshape.66) | data formatting | bytes 1048576 | tf_op jit(solution)/shard_map/reshape | solution.py:126
  108.5 5.8 %all-to-all-start.3 = ((bf16[64,2,2048]{2,1,0:T(2,128)(2,1)}), bf16[64,2,2048]{2,1,0:T(2,128)(2,1)S(1)}, u32[]{:S(2)}, u32[]{:S(2)}) async-start(bf16[64,2,2048]{2,1,0:T(2,128)(2,1)} %bitcast.33), calls=%async_computation.3 | async-start | bytes 1048576 | tf_op jit(solution)/shard_map/all_to_all | solution.py:128
  114.2 0.1 reshape.59
  114.4 4.2 %collective-permute-start.5 = (f32[20,32]{0,1:T(8,128)S(1)}, f32[20,32]{0,1:T(8,128)S(1)}, u32[]{:S(2)}, u32[]{:S(2)}) collective-permute-start(f32[20,32]{0,1:T(8,128)S(1)} %bitcast.118), channel_id=1, source_target_pairs={{0,36},{4,32},{8,44},{12,40},{16,52},{20,48},{24,60},{28,56},{32,4... | collective-permute-start | bytes 7688 | tf_op jit(solution)/shard_map/ppermute | solution.py:46
  118.6 2.1 %collective-permute-start.4 = (f32[20,32]{0,1:T(8,128)S(1)}, f32[20,32]{0,1:T(8,128)S(1)}, u32[]{:S(2)}, u32[]{:S(2)}) collective-permute-start(f32[20,32]{0,1:T(8,128)S(1)} %bitcast.116), channel_id=1, source_target_pairs={{0,32},{4,36},{8,40},{12,44},{16,48},{20,52},{24,56},{28,60},{32,0... | collective-permute-start | bytes 7688 | tf_op jit(solution)/shard_map/ppermute | solution.py:46
  120.7 2.1 %collective-permute-start.3 = (f32[20,32]{0,1:T(8,128)S(1)}, f32[20,32]{0,1:T(8,128)S(1)}, u32[]{:S(2)}, u32[]{:S(2)}) collective-permute-start(f32[20,32]{0,1:T(8,128)S(1)} %bitcast.114), channel_id=1, source_target_pairs={{0,4},{4,0},{8,12},{12,8},{16,20},{20,16},{24,28},{28,24},{32,36},... | collective-permute-start | bytes 7688 | tf_op jit(solution)/shard_map/ppermute | solution.py:46
  122.9 0.7 collective-permute-done.4
  123.6 0.2 collective-permute-done.3
  124.0 0.7 copy.175
  124.7 6.8 %all-to-all-done.3 = bf16[64,2,2048]{2,1,0:T(2,128)(2,1)S(1)} async-done(((bf16[64,2,2048]{2,1,0:T(2,128)(2,1)}), bf16[64,2,2048]{2,1,0:T(2,128)(2,1)S(1)}, u32[]{:S(2)}, u32[]{:S(2)}) %all-to-all-start.3) | async-done | bytes 524320 | tf_op jit(solution)/shard_map/all_to_all | solution.py:128
  131.5 0.7 reduce_sum.22
  132.4 0.2 fusion.12
  132.6 0.7 copy.176
  (44 shorter events, 1.1 us)
Async XLA Ops:
  2.3 26.9 %all-to-all-start = ((bf16[32,64,128]{2,1,0:T(8,128)(2,1)}), bf16[32,64,128]{2,1,0:T(8,128)(2,1)S(1)}, u32[]{:S(2)}, u32[]{:S(2)}) async-start(bf16[32,64,128]{2,1,0:T(8,128)(2,1)} %broadcast_in_dim.22), calls=%async_computation | async-start | bytes 1048576 | tf_op jit(solution)/shard_map/all_to_all | solution.py:66
  14.9 9.9 %collective-permute-start = (bf16[21,64,128]{2,0,1:T(8,128)(2,1)S(1)}, bf16[21,64,128]{2,0,1:T(8,128)(2,1)}, u32[]{:S(2)}, u32[]{:S(2)}) collective-permute-start(bf16[21,64,128]{2,0,1:T(8,128)(2,1)S(1)} %pad_maximum_fusion), channel_id=1, source_target_pairs={{0,4},{4,0},{8,12},{12,8},{16,20},{20,16},{24,28},{28,24},{32,36},... | collective-permute-start | bytes 1032200 | tf_op jit(solution)/shard_map/ppermute | solution.py:46
  29.2 19.6 %copy-start.3 = (bf16[1,64,128]{2,1,0:T(8,128)(2,1)S(1)}, bf16[1,64,128]{2,1,0:T(8,128)(2,1)}, u32[]{:S(2)}) copy-start(bf16[1,64,128]{2,1,0:T(8,128)(2,1)} %param.9) | copy-start | bytes 49156
  29.2 50.5 %all-to-all-start.1 = ((bf16[16,40,2048]{2,1,0:T(8,128)(2,1)}), bf16[16,40,2048]{2,1,0:T(8,128)(2,1)S(1)}, u32[]{:S(2)}, u32[]{:S(2)}) async-start(bf16[16,40,2048]{2,1,0:T(8,128)(2,1)} %bitcast.93), calls=%async_computation.1 | async-start | bytes 5242880 | tf_op jit(solution)/shard_map/all_to_all | solution.py:78
  33.3 10.4 %collective-permute-start.1 = (bf16[21,64,128]{2,0,1:T(8,128)(2,1)S(1)}, bf16[21,64,128]{2,0,1:T(8,128)(2,1)}, u32[]{:S(2)}, u32[]{:S(2)}) collective-permute-start(bf16[21,64,128]{2,0,1:T(8,128)(2,1)S(1)} %pad_maximum_fusion), channel_id=1, source_target_pairs={{0,32},{4,36},{8,40},{12,44},{16,48},{20,52},{24,56},{28,60},{32,0... | collective-permute-start | bytes 1032200 | tf_op jit(solution)/shard_map/ppermute | solution.py:46
  43.7 8.1 %collective-permute-start.2 = (bf16[21,64,128]{2,0,1:T(8,128)(2,1)}, bf16[21,64,128]{2,0,1:T(8,128)(2,1)}, u32[]{:S(2)}, u32[]{:S(2)}) collective-permute-start(bf16[21,64,128]{2,0,1:T(8,128)(2,1)} %collective-permute-done.1), channel_id=1, source_target_pairs={{0,4},{4,0},{8,12},{12,8},{16,20},{20,16},{24,28},{28,24},{32,36},... | collective-permute-start | bytes 1032200 | tf_op jit(solution)/shard_map/ppermute | solution.py:46
  51.8 2.1 %copy-start.1 = (bf16[1,64,128]{1,2,0:T(8,128)(2,1)S(1)}, bf16[1,64,128]{1,2,0:T(8,128)(2,1)}, u32[]{:S(2)}) copy-start(bf16[1,64,128]{1,2,0:T(8,128)(2,1)} %copy.149) | copy-start | bytes 49156
  77.6 26.1 %copy-start = (bf16[4,148,128]{2,1,0:T(8,128)(2,1)}, bf16[4,148,128]{2,1,0:T(8,128)(2,1)S(1)}, u32[]{:S(2)}) copy-start(bf16[4,148,128]{2,1,0:T(8,128)(2,1)S(1)} %all-gather.1) | copy-start | bytes 454660
  79.8 24.7 %collective-permute-start.6 = (bf16[640,2048]{1,0:T(8,128)(2,1)S(1)}, bf16[640,2048]{1,0:T(8,128)(2,1)}, u32[]{:S(2)}, u32[]{:S(2)}) collective-permute-start(bf16[640,2048]{1,0:T(8,128)(2,1)S(1)} %bitcast.91), channel_id=1, source_target_pairs={{0,4},{4,0},{8,12},{12,8},{16,20},{20,16},{24,28},{28,24},{32,36},... | collective-permute-start | bytes 7864328 | tf_op jit(solution)/shard_map/ppermute | solution.py:46
  107.1 25.3 %slice-start = ((bf16[4,148,128]{2,1,0:T(8,128)(2,1)}), bf16[4,64,128]{2,1,0:T(8,128)(2,1)S(1)}, s32[]{:S(2)}) async-start(bf16[4,148,128]{2,1,0:T(8,128)(2,1)} %copy-done), calls=%async_computation.4 | async-start | bytes 131072 | tf_op jit(solution)/shard_map/slice | solution.py:97
  107.1 25.3 %copy-start.2 = (bf16[1,64,128]{1,2,0:T(8,128)(2,1)S(1)}, bf16[1,64,128]{1,2,0:T(8,128)(2,1)}, u32[]{:S(2)}) copy-start(bf16[1,64,128]{1,2,0:T(8,128)(2,1)} %copy.149) | copy-start | bytes 49156
  108.5 23.0 %all-to-all-start.3 = ((bf16[64,2,2048]{2,1,0:T(2,128)(2,1)}), bf16[64,2,2048]{2,1,0:T(2,128)(2,1)S(1)}, u32[]{:S(2)}, u32[]{:S(2)}) async-start(bf16[64,2,2048]{2,1,0:T(2,128)(2,1)} %bitcast.33), calls=%async_computation.3 | async-start | bytes 1048576 | tf_op jit(solution)/shard_map/all_to_all | solution.py:128
  114.4 8.5 %collective-permute-start.5 = (f32[20,32]{0,1:T(8,128)S(1)}, f32[20,32]{0,1:T(8,128)S(1)}, u32[]{:S(2)}, u32[]{:S(2)}) collective-permute-start(f32[20,32]{0,1:T(8,128)S(1)} %bitcast.118), channel_id=1, source_target_pairs={{0,36},{4,32},{8,44},{12,40},{16,52},{20,48},{24,60},{28,56},{32,4... | collective-permute-start | bytes 7688 | tf_op jit(solution)/shard_map/ppermute | solution.py:46
  118.6 5.0 %collective-permute-start.4 = (f32[20,32]{0,1:T(8,128)S(1)}, f32[20,32]{0,1:T(8,128)S(1)}, u32[]{:S(2)}, u32[]{:S(2)}) collective-permute-start(f32[20,32]{0,1:T(8,128)S(1)} %bitcast.116), channel_id=1, source_target_pairs={{0,32},{4,36},{8,40},{12,44},{16,48},{20,52},{24,56},{28,60},{32,0... | collective-permute-start | bytes 7688 | tf_op jit(solution)/shard_map/ppermute | solution.py:46
  120.7 3.1 %collective-permute-start.3 = (f32[20,32]{0,1:T(8,128)S(1)}, f32[20,32]{0,1:T(8,128)S(1)}, u32[]{:S(2)}, u32[]{:S(2)}) collective-permute-start(f32[20,32]{0,1:T(8,128)S(1)} %bitcast.114), channel_id=1, source_target_pairs={{0,4},{4,0},{8,12},{12,8},{16,20},{20,16},{24,28},{28,24},{32,36},... | collective-permute-start | bytes 7688 | tf_op jit(solution)/shard_map/ppermute | solution.py:46
